TPU v7x, 32 devices: a whole 2x2x4 slice. The times are simulated.
32 devices in a mesh: groups: 2 (over y), rows: 4 (over z), cols: 2 (over x), maps: 2 (over core).
Axes of the slice: x: 2, y: 2, z: 4, core: 2. Of those that a mesh axis runs over, the one named last changes fastest.
Arguments:
- drivers: bfloat16 [4, 16, 512, 256], P(('groups', 'maps'), None, 'rows', 'cols'), parts along dimension 0, may hold values from -6 to 6
- observed: bfloat16 [4, 512, 256], P(('groups', 'maps'), 'rows', 'cols'), parts along dimension 0, may hold values from 0.099609375 to 3
- confidence: bfloat16 [4, 512, 256], P(('groups', 'maps'), 'rows', 'cols'), parts along dimension 0, may hold values from 0.19921875 to 2
- land_mask: int32 [1024, 256], P(('groups', 'rows'), 'cols'), parts along dimension 0, may hold values from 0 to 1, as said below
- ownership: int32 [1024, 4], P(('groups', 'rows'), 'cols'), parts along dimension 0, may hold values from -1 to 7, as said below
- first_layer: bfloat16 [16, 128], replicated, may hold values from -1.5 to 1.5
- second_layer: bfloat16 [128, 128], replicated, may hold values from -0.5 to 0.5
- output_layer: bfloat16 [128], replicated, may hold values from -0.5 to 0.5
Outputs:
- first_gradient: float32 [32, 128], P('groups'), parts along dimension 0
- second_gradient: float32 [256, 128], P('groups'), parts along dimension 0
- output_gradient: float32 [256], P('groups'), parts along dimension 0
- source_scaling: float32 [4, 512, 256], P(('groups', 'maps'), 'rows', 'cols'), parts along dimension 0
- target_scaling: float32 [4, 512, 256], P(('groups', 'maps'), 'rows', 'cols'), parts along dimension 0
There are 2 independent parts, one for each index of `groups`. A program takes and returns all parts, laid end to end along the dimension named above; an argument that names none is the same for every part. Nothing has to cross between parts.
Inputs may be any that keep to these rules, and one draw needn't show every extreme that they name: `ownership`: -1 marks a block without land. Every device of rows and cols owns exactly 96 land blocks of the slab, and at most 32 blocks of one device's tile; some tile gives 32 blocks to one owner. `land_mask`: land cells lie only in blocks whose ownership is not -1, and every such block holds one or more.
All inputs are finite; a program needn't handle non-finite values.
Results may differ from a plain program's by a relative error of at most 0.0013.
Values may be sent and summed in bfloat16 or wider, within the bound.
No kernel may reach another device: no remote copies, remote signals or barrier semaphores. Data moves between devices by JAX's collectives and lax.ppermute only.
A program may use at most 64 MiB of HBM per device.

v0:
```python
import jax
import jax.numpy as jnp
from jax import lax
from jax.sharding import PartitionSpec as P

RADIUS = 24
ITERS = 2


HIGHEST = lax.Precision.HIGHEST
BACKGROUND = 0.1


def extended(cells, sides, width):
    for axis, dim in sides:
        count = lax.axis_size(axis)
        ends = count - 1
        head = lax.slice_in_dim(cells, 0, width, axis=dim)
        tail = lax.slice_in_dim(cells, cells.shape[dim] - width, cells.shape[dim], axis=dim)
        cells = jnp.concatenate(
            [
                lax.ppermute(tail, axis, [(i, (i + 1) % count) for i in range(ends)]),
                cells,
                lax.ppermute(head, axis, [((i + 1) % count, i) for i in range(ends)]),
            ],
            axis=dim,
        )
    return cells


def silu_slope(value):
    logistic = jax.nn.sigmoid(value)
    return logistic * (1.0 + value * (1.0 - logistic))


def imitate(inputs, targets, first_layer, second_layer, output_layer):
    pre_first = jnp.einsum("nmfb,fh->nmbh", inputs, first_layer, preferred_element_type=jnp.float32)
    hidden_first = jax.nn.silu(pre_first).astype(jnp.bfloat16)
    pre_second = jnp.einsum(
        "nmbh,hk->nmbk", hidden_first, second_layer, preferred_element_type=jnp.float32
    )
    hidden_second = jax.nn.silu(pre_second).astype(jnp.bfloat16)
    score = jnp.einsum(
        "nmbk,k->nmb", hidden_second, output_layer, preferred_element_type=jnp.float32
    )
    imitated = jax.nn.softplus(score)
    observed_part = targets[:, :, 0].astype(jnp.float32)
    weighted_part = targets[:, :, 1].astype(jnp.float32)
    delta_score = weighted_part * (imitated - observed_part) * jax.nn.sigmoid(score)
    output_grad = jnp.einsum(
        "nmb,nmbk->k", delta_score, hidden_second, preferred_element_type=jnp.float32
    )
    delta_second = (
        delta_score[..., None] * output_layer.astype(jnp.float32) * silu_slope(pre_second)
    ).astype(jnp.bfloat16)
    second_grad = jnp.einsum(
        "nmbh,nmbk->hk", hidden_first, delta_second, preferred_element_type=jnp.float32
    )
    back_first = jnp.einsum(
        "nmbk,hk->nmbh", delta_second, second_layer, preferred_element_type=jnp.float32
    )
    delta_first = (back_first * silu_slope(pre_first)).astype(jnp.bfloat16)
    first_grad = jnp.einsum(
        "nmfb,nmbh->fh", inputs, delta_first, preferred_element_type=jnp.float32
    )
    return (imitated, (first_grad, second_grad, output_grad))


def band(count_out, count_in):
    offsets = jnp.arange(-RADIUS, RADIUS + 1).astype(jnp.float32)
    norm_total = jnp.sum(jnp.exp(-4.5 * offsets * offsets / (RADIUS * RADIUS)))
    out_index = lax.broadcasted_iota(jnp.int32, (count_out, count_in), 0)
    in_index = lax.broadcasted_iota(jnp.int32, (count_out, count_in), 1)
    distance = in_index - out_index
    offset = (distance - RADIUS).astype(jnp.float32)
    values = jnp.exp(-4.5 * offset * offset / (RADIUS * RADIUS)) / norm_total
    return jnp.where((distance >= 0) & (distance <= 2 * RADIUS), values, 0.0)


def smooth(field, band_rows, band_cols):
    padded = extended(field, (("rows", 1),), RADIUS)
    along_rows = jnp.einsum("ij,mjc->mic", band_rows, padded, precision=HIGHEST)
    widened = extended(along_rows, (("cols", 2),), RADIUS)
    result = jnp.einsum("mij,cj->mic", widened, band_cols, precision=HIGHEST)
    return result


def local(
    drivers, observed, confidence, land_mask, ownership, first_layer, second_layer, output_layer
):
    map_count, feature_count, tile_rows, tile_cols = drivers.shape
    per_row = ownership.shape[1]
    block_width = tile_cols // per_row
    block_count = tile_rows * per_row
    mask_float = land_mask.astype(jnp.float32)
    weighted = (confidence.astype(jnp.float32) * mask_float[None]).astype(jnp.bfloat16)
    blocks = (
        drivers.reshape(map_count, feature_count, tile_rows, per_row, block_width)
        .transpose(2, 3, 0, 1, 4)
        .reshape(block_count, map_count, feature_count, block_width)
    )
    paired = jnp.stack([observed, weighted], axis=1)
    targets = (
        paired.reshape(map_count, 2, tile_rows, per_row, block_width)
        .transpose(2, 3, 0, 1, 4)
        .reshape(block_count, map_count, 2, block_width)
    )
    row_devices = lax.axis_size("rows")
    col_devices = lax.axis_size("cols")
    owner_total = row_devices * col_devices
    capacity = max(2, (block_count + owner_total - 1) // owner_total)
    owned = capacity * (block_count * 7 // (16 * capacity))
    slots = owner_total * capacity
    owners_flat = ownership.reshape(block_count)
    onehot = (owners_flat[:, None] == jnp.arange(owner_total, dtype=jnp.int32)[None, :]).astype(
        jnp.int32
    )
    earlier = jnp.cumsum(onehot, axis=0) - onehot
    rank = jnp.sum(earlier * onehot, axis=1)
    landed = owners_flat >= 0
    slot_of_block = jnp.where(landed, owners_flat * capacity + rank, slots)
    matches = (slot_of_block[:, None] == jnp.arange(slots, dtype=jnp.int32)[None, :]).astype(
        jnp.int32
    )
    live = jnp.sum(matches, axis=0)
    source_block = jnp.sum(matches * jnp.arange(block_count, dtype=jnp.int32)[:, None], axis=0)
    sent_inputs = jnp.where(
        live[:, None, None, None] > 0,
        jnp.take(blocks, source_block, axis=0),
        jnp.zeros((), jnp.bfloat16),
    )
    sent_targets = jnp.where(
        live[:, None, None, None] > 0,
        jnp.take(targets, source_block, axis=0),
        jnp.zeros((), jnp.bfloat16),
    )
    sent_inputs = sent_inputs.reshape(
        owner_total, capacity, map_count * feature_count * block_width
    )
    sent_targets = sent_targets.reshape(owner_total, capacity, map_count * 2 * block_width)
    sent_flags = live.reshape(owner_total, capacity)
    arrived = (
        lax.all_to_all(sent_inputs, ("rows", "cols"), split_axis=0, concat_axis=0, tiled=True),
        lax.all_to_all(sent_targets, ("rows", "cols"), split_axis=0, concat_axis=0, tiled=True),
        lax.all_to_all(sent_flags, ("rows", "cols"), split_axis=0, concat_axis=0, tiled=True),
    )
    got_inputs = arrived[0].reshape(slots, map_count, feature_count, block_width)
    got_targets = arrived[1].reshape(slots, map_count, 2, block_width)
    got_live = arrived[2].reshape(slots)
    position = jnp.cumsum(got_live) - 1
    picks = (
        (position[None, :] == jnp.arange(owned, dtype=jnp.int32)[:, None]) & (got_live[None, :] > 0)
    ).astype(jnp.int32)
    chosen_slot = jnp.sum(picks * jnp.arange(slots, dtype=jnp.int32)[None, :], axis=1)
    computed, grads = imitate(
        jnp.take(got_inputs, chosen_slot, axis=0),
        jnp.take(got_targets, chosen_slot, axis=0),
        first_layer,
        second_layer,
        output_layer,
    )
    returned = jnp.where(
        got_live[:, None, None] > 0,
        jnp.take(computed, jnp.clip(position, 0, owned - 1), axis=0),
        0.0,
    )
    returned = returned.reshape(owner_total, capacity, map_count * block_width)
    back = lax.all_to_all(returned, ("rows", "cols"), split_axis=0, concat_axis=0, tiled=True)
    back = back.reshape(slots, map_count, block_width)
    imitated = jnp.where(
        landed[:, None, None], jnp.take(back, jnp.clip(slot_of_block, 0, slots - 1), axis=0), 0.0
    )
    weight_part = jnp.sum(weighted.astype(jnp.float32))
    first_sum, second_sum, output_sum, weight_total = lax.psum(
        (grads[0], grads[1], grads[2], weight_part), ("rows", "cols", "maps")
    )
    imitated_map = (
        imitated.reshape(tile_rows, per_row, map_count, block_width)
        .transpose(2, 0, 1, 3)
        .reshape(map_count, tile_rows, tile_cols)
    )
    source = mask_float[None] * imitated_map + BACKGROUND
    target = mask_float[None] * observed.astype(jnp.float32) + BACKGROUND
    cell_total = tile_rows * tile_cols * lax.axis_size("rows") * lax.axis_size("cols")
    source_mass, target_mass = lax.psum(
        (jnp.sum(source, axis=(1, 2)), jnp.sum(target, axis=(1, 2))), ("rows", "cols")
    )
    source = source / (source_mass / cell_total)[:, None, None]
    target = target / (target_mass / cell_total)[:, None, None]
    band_rows = band(tile_rows, tile_rows + 2 * RADIUS)
    band_cols = band(tile_cols, tile_cols + 2 * RADIUS)
    target_scaling = jnp.ones_like(source)
    source_scaling = source
    for step in range(ITERS):
        source_scaling = source / smooth(target_scaling, band_rows, band_cols)
        target_scaling = target / smooth(source_scaling, band_rows, band_cols)
    return (
        first_sum / weight_total,
        second_sum / weight_total,
        output_sum / weight_total,
        source_scaling,
        target_scaling,
    )


def solution(mesh):
    in_specs = (
        P(("groups", "maps"), None, "rows", "cols"),
        P(("groups", "maps"), "rows", "cols"),
        P(("groups", "maps"), "rows", "cols"),
        P(("groups", "rows"), "cols"),
        P(("groups", "rows"), "cols"),
        P(),
        P(),
        P(),
    )
    out_specs = (
        P("groups", None),
        P("groups", None),
        P("groups"),
        P(("groups", "maps"), "rows", "cols"),
        P(("groups", "maps"), "rows", "cols"),
    )
    return jax.shard_map(local, mesh=mesh, in_specs=in_specs, out_specs=out_specs, check_vma=False)
```

profile of v0, /device:TPU:0, one launch (start us, length us, event | category | flops | bytes accessed | tf_op | source)
XLA Modules:
  0.0 275.1 jit_solution(18373256191185227951)
XLA Ops:
  7.2 4.9 %collective-permute-start = (f32[1,24,128]{2,1,0:T(8,128)S(1)}, f32[1,24,128]{2,1,0:T(8,128)S(1)}, u32[]{:S(2)}, u32[]{:S(2)}) collective-permute-start(f32[1,24,128]{2,1,0:T(8,128)S(1)} %broadcast.422), channel_id=1, source_target_pairs={{0,4},{4,8},{8,12},{1,5},{5,9},{9,13},{2,6},{6,10},{10,14},{3,7},{... | collective-permute-start | bytes 36872 | tf_op jit(solution)/shard_map/ppermute | solution.py:22
  12.1 1.3 collective-permute-start.1
  13.4 0.8 copy.52
  16.3 6.9 %all-to-all-start = ((s32[8,1,32]{2,1,0:T(1,128)}), s32[8,1,32]{2,1,0:T(1,128)S(1)}, u32[]{:S(2)}, u32[]{:S(2)}) async-start(s32[8,1,32]{2,1,0:T(1,128)} %all_to_all.15), calls=%async_computation | async-start | bytes 8192 | tf_op jit(solution)/shard_map/all_to_all | solution.py:145
  23.2 0.7 broadcast_multiply_fusion
  24.6 1.3 copy.55
  26.0 1.6 copy.56
  27.6 0.9 gather_fusion
  28.5 0.7 gather.35
  29.5 0.7 convert_reduce_fusion.1
  30.4 0.9 gather_fusion.2
  31.5 0.9 select_select_fusion
  32.4 0.8 select_select_fusion.2
  34.5 0.7 broadcast_in_dim.160
  35.3 0.7 broadcast_in_dim.162
  37.3 6.0 %all-to-all-start.2 = ((bf16[8,32,128]{2,1,0:T(8,128)(2,1)}), bf16[8,32,128]{2,1,0:T(8,128)(2,1)S(1)}, u32[]{:S(2)}, u32[]{:S(2)}) async-start(bf16[8,32,128]{2,1,0:T(8,128)(2,1)} %select_select_fusion.2), calls=%async_computation.2 | async-start | bytes 131072 | tf_op jit(solution)/shard_map/all_to_all | solution.py:144
  46.8 3.4 %all-to-all-done.2 = bf16[8,32,128]{2,1,0:T(8,128)(2,1)S(1)} async-done(((bf16[8,32,128]{2,1,0:T(8,128)(2,1)}), bf16[8,32,128]{2,1,0:T(8,128)(2,1)S(1)}, u32[]{:S(2)}, u32[]{:S(2)}) %all-to-all-start.2) | async-done | bytes 65568 | tf_op jit(solution)/shard_map/all_to_all | solution.py:144
  50.2 3.5 %all-to-all-start.1 = ((bf16[8,32,1024]{2,1,0:T(8,128)(2,1)}), bf16[8,32,1024]{2,1,0:T(8,128)(2,1)S(1)}, u32[]{:S(2)}, u32[]{:S(2)}) async-start(bf16[8,32,1024]{2,1,0:T(8,128)(2,1)} %select_select_fusion), calls=%async_computation.1 | async-start | bytes 1048576 | tf_op jit(solution)/shard_map/all_to_all | solution.py:143
  53.7 1.1 convolution_bitcast_fusion.3
  55.5 4.4 %collective-permute-start.2 = (f32[1,128,24]{1,2,0:T(8,128)}, f32[1,128,24]{1,2,0:T(8,128)}, u32[]{:S(2)}, u32[]{:S(2)}) collective-permute-start(f32[1,128,24]{1,2,0:T(8,128)} %get-tuple-element.31), channel_id=1, source_target_pairs={{0,2},{1,3},{4,6},{5,7},{8,10},{9,11},{12,14},{13,15},{16,18},{17,... | collective-permute-start | bytes 36872 | tf_op jit(solution)/shard_map/ppermute | solution.py:22
  59.9 1.3 collective-permute-start.3
  61.3 0.7 gather_fusion.3
  62.2 3.6 %all-to-all-done.1 = bf16[8,32,1024]{2,1,0:T(8,128)(2,1)S(1)} async-done(((bf16[8,32,1024]{2,1,0:T(8,128)(2,1)}), bf16[8,32,1024]{2,1,0:T(8,128)(2,1)S(1)}, u32[]{:S(2)}, u32[]{:S(2)}) %all-to-all-start.1) | async-done | bytes 524320 | tf_op jit(solution)/shard_map/all_to_all | solution.py:143
  67.2 2.7 multiply_convert_fusion.3
  69.9 1.0 multiply_convert_fusion.2
  71.1 1.3 fusion.77
  72.4 0.7 gather_fusion.4
  73.2 0.8 select_select_fusion.1
  74.0 0.8 reshape.575
  74.8 3.7 %all-to-all-start.3 = ((f32[8,1,2048]{2,1,0:T(1,128)}), f32[8,1,2048]{2,1,0:T(1,128)S(1)}, u32[]{:S(2)}, u32[]{:S(2)}) async-start(f32[8,1,2048]{2,1,0:T(1,128)} %reshape.575), calls=%async_computation.3 | async-start | bytes 131072 | tf_op jit(solution)/shard_map/all_to_all | solution.py:168
  78.5 3.2 %multiply_convert_fusion.1 = bf16[96,64,128]{2,1,0:T(8,128)(2,1)} fusion(f32[96,64,128]{2,1,0:T(8,128)S(1)} %get-tuple-element.43, f32[128]{0:T(128)} %convert_element_type.79, f32[96,64]{1,0:T(8,128)S(1)} %get-tuple-element.34), kind=kLoop, calls=%fused_computation.7 | loop fusion | flops 7864320 | bytes 4743680 | tf_op jit(solution)/shard_map/convert_element_type | solution.py:55
  81.7 3.6 %all-to-all-done.3 = f32[8,1,2048]{2,1,0:T(1,128)S(1)} async-done(((f32[8,1,2048]{2,1,0:T(1,128)}), f32[8,1,2048]{2,1,0:T(1,128)S(1)}, u32[]{:S(2)}, u32[]{:S(2)}) %all-to-all-start.3) | async-done | bytes 65568 | tf_op jit(solution)/shard_map/all_to_all | solution.py:168
  85.8 0.8 reduce.11
  86.7 0.9 gather_fusion.5
  88.3 19.0 %all-reduce.1 = (f32[1]{0:T(128)}, f32[1]{0:T(128)}) all-reduce(f32[1]{0:T(128)} %bitcast.36, f32[1]{0:T(128)} %bitcast.38), channel_id=1, replica_groups=mesh['groups'=2,'rows'=4,'cols'=2,'maps'=2] {'rows','cols'}, use_global_device_ids=true, to_apply=%region_14.15 | all-reduce | flops 2 | bytes 16 | tf_op jit(solution)/shard_map/psum | solution.py:185
  108.0 1.8 fusion.6
  109.8 1.3 collective-permute-start.4
  111.1 1.3 collective-permute-start.5
  112.4 4.1 %fusion.7 = f32[16,128]{1,0:T(8,128)S(1)} fusion(f32[96,64,128]{2,1,0:T(8,128)} %get-tuple-element.41, bf16[96,64,128]{2,1,0:T(8,128)(2,1)} %multiply_convert_fusion.1, bf16[96,16,64]{2,1,0:T(8,128)(2,1)} %copy-done.4, pred[96]{0:T(512)(128)(4,1)S(1)} %copy-done.18, bf16[128,128]{1,0:T(8,128)(2,1)S(1)} %copy-done), kind=kOutput, calls=%fused_computation.28 | convolution fusion | flops 233668608 | bytes 4956256 | tf_op jit(solution)/shard_map/nmfb,nmbh->fh/dot_general | solution.py:63
  116.7 2.0 convolution_bitcast_fusion.2
  118.7 2.9 %collective-permute-start.6 = (f32[1,128,24]{1,2,0:T(8,128)S(1)}, f32[1,128,24]{1,2,0:T(8,128)S(1)}, u32[]{:S(2)}, u32[]{:S(2)}) collective-permute-start(f32[1,128,24]{1,2,0:T(8,128)S(1)} %get-tuple-element.26), channel_id=1, source_target_pairs={{0,2},{1,3},{4,6},{5,7},{8,10},{9,11},{12,14},{13,15},{16,18},{17,... | collective-permute-start | bytes 36872 | tf_op jit(solution)/shard_map/ppermute | solution.py:22
  121.6 1.3 collective-permute-start.7
  122.9 2.7 convolution_bitcast_fusion.4
  126.2 1.0 collective-permute-done.7
  127.2 1.9 fusion.8
  129.1 4.4 %collective-permute-start.8 = (f32[1,24,128]{2,1,0:T(8,128)S(1)}, f32[1,24,128]{2,1,0:T(8,128)S(1)}, u32[]{:S(2)}, u32[]{:S(2)}) collective-permute-start(f32[1,24,128]{2,1,0:T(8,128)S(1)} %get-tuple-element.24), channel_id=1, source_target_pairs={{0,4},{4,8},{8,12},{1,5},{5,9},{9,13},{2,6},{6,10},{10,14},{3,7},{... | collective-permute-start | bytes 36872 | tf_op jit(solution)/shard_map/ppermute | solution.py:22
  133.6 1.3 collective-permute-start.9
  135.2 31.1 %all-reduce = (f32[16,128]{1,0:T(8,128)S(1)}, f32[]{:T(128)}, f32[128]{0:T(128)S(1)}) all-reduce(f32[16,128]{1,0:T(8,128)S(1)} %fusion.7, f32[]{:T(128)} %get-tuple-element.16, f32[128]{0:T(128)S(1)} %convolution_bitcast_fusion.5), channel_id=1, replica_groups=mesh['groups'=2,'rows'=4,'cols'=2,'maps'=2] {'rows','cols','maps'}, use_global_device_ids=true, to_apply=%region_8.9 | all-reduce | flops 2177 | bytes 17416 | tf_op jit(solution)/shard_map/psum | solution.py:174
  166.3 1.1 convolution_bitcast_fusion.1
  167.4 1.3 collective-permute-start.10
  168.7 1.3 collective-permute-start.11
  170.0 1.1 broadcast_divide_fusion.1
  171.1 3.1 %collective-permute-done.11 = f32[1,128,24]{1,2,0:T(8,128)S(1)} collective-permute-done((f32[1,128,24]{1,2,0:T(8,128)S(1)}, f32[1,128,24]{1,2,0:T(8,128)S(1)}, u32[]{:S(2)}, u32[]{:S(2)}) %collective-permute-start.11) | collective-permute-done | bytes 12320 | tf_op jit(solution)/shard_map/ppermute | solution.py:24
  174.3 1.1 fusion.3
  175.4 1.3 collective-permute-start.12
  176.7 1.3 collective-permute-start.13
  178.0 1.1 broadcast_divide_fusion.2
  179.1 3.2 %collective-permute-done.13 = f32[1,24,128]{2,1,0:T(8,128)S(1)} collective-permute-done((f32[1,24,128]{2,1,0:T(8,128)S(1)}, f32[1,24,128]{2,1,0:T(8,128)S(1)}, u32[]{:S(2)}, u32[]{:S(2)}) %collective-permute-start.13) | collective-permute-done | bytes 12320 | tf_op jit(solution)/shard_map/ppermute | solution.py:24
  182.2 1.1 convolution_bitcast_fusion
  183.3 1.6 collective-permute-start.14
  185.0 1.3 collective-permute-start.15
  186.3 78.2 %all-reduce.4.cloned.1.call-done = f32[128,128]{1,0:T(8,128)} async-done(((f32[128,128]{1,0:T(8,128)}), f32[128,128]{1,0:T(8,128)}) %all-reduce.4.cloned.1.call-update) | async-done | bytes 65552 | tf_op jit(solution)/shard_map/psum | solution.py:174
  264.5 2.0 broadcast_divide_fusion
  266.5 1.7 fusion.9
  (133 shorter events, 14.1 us)
Async XLA Ops:
  7.2 62.7 %copy-start = (bf16[128,128]{1,0:T(8,128)(2,1)S(1)}, bf16[128,128]{1,0:T(8,128)(2,1)}, u32[]{:S(2)}) copy-start(bf16[128,128]{1,0:T(8,128)(2,1)} %param.14) | copy-start | bytes 98308
  7.2 46.5 %collective-permute-start = (f32[1,24,128]{2,1,0:T(8,128)S(1)}, f32[1,24,128]{2,1,0:T(8,128)S(1)}, u32[]{:S(2)}, u32[]{:S(2)}) collective-permute-start(f32[1,24,128]{2,1,0:T(8,128)S(1)} %broadcast.422), channel_id=1, source_target_pairs={{0,4},{4,8},{8,12},{1,5},{5,9},{9,13},{2,6},{6,10},{10,14},{3,7},{... | collective-permute-start | bytes 36872 | tf_op jit(solution)/shard_map/ppermute | solution.py:22
  12.1 41.6 %collective-permute-start.1 = (f32[1,24,128]{2,1,0:T(8,128)S(1)}, f32[1,24,128]{2,1,0:T(8,128)S(1)}, u32[]{:S(2)}, u32[]{:S(2)}) collective-permute-start(f32[1,24,128]{2,1,0:T(8,128)S(1)} %broadcast.422), channel_id=1, source_target_pairs={{4,0},{8,4},{12,8},{5,1},{9,5},{13,9},{6,2},{10,6},{14,10},{7,3},{... | collective-permute-start | bytes 36872 | tf_op jit(solution)/shard_map/ppermute | solution.py:24
  16.3 21.0 %all-to-all-start = ((s32[8,1,32]{2,1,0:T(1,128)}), s32[8,1,32]{2,1,0:T(1,128)S(1)}, u32[]{:S(2)}, u32[]{:S(2)}) async-start(s32[8,1,32]{2,1,0:T(1,128)} %all_to_all.15), calls=%async_computation | async-start | bytes 8192 | tf_op jit(solution)/shard_map/all_to_all | solution.py:145
  24.6 4.7 %copy-start.6 = (bf16[1,128,128]{2,1,0:T(8,128)(2,1)S(1)}, bf16[1,128,128]{2,1,0:T(8,128)(2,1)}, u32[]{:S(2)}) copy-start(bf16[1,128,128]{2,1,0:T(8,128)(2,1)} %param.9) | copy-start | bytes 98308
  24.6 4.8 %copy-start.5 = (s32[128,128]{1,0:T(8,128)S(1)}, s32[128,128]{1,0:T(8,128)}, u32[]{:S(2)}) copy-start(s32[128,128]{1,0:T(8,128)} %param.11) | copy-start | bytes 196612
  24.6 4.8 %copy-start.10 = (bf16[1,128,128]{2,1,0:T(8,128)(2,1)S(1)}, bf16[1,128,128]{2,1,0:T(8,128)(2,1)}, u32[]{:S(2)}) copy-start(bf16[1,128,128]{2,1,0:T(8,128)(2,1)} %param.10) | copy-start | bytes 98308
  27.6 8.4 %copy-start.16 = (bf16[128]{0:T(256)(128)(2,1)S(1)}, bf16[128]{0:T(256)(128)(2,1)}, u32[]{:S(2)}) copy-start(bf16[128]{0:T(256)(128)(2,1)} %param.15) | copy-start | bytes 772
  31.5 35.7 %copy-start.19 = (bf16[16,128]{1,0:T(8,128)(2,1)S(1)}, bf16[16,128]{1,0:T(8,128)(2,1)}, u32[]{:S(2)}) copy-start(bf16[16,128]{1,0:T(8,128)(2,1)} %param.13) | copy-start | bytes 12292
  37.3 12.9 %all-to-all-start.2 = ((bf16[8,32,128]{2,1,0:T(8,128)(2,1)}), bf16[8,32,128]{2,1,0:T(8,128)(2,1)S(1)}, u32[]{:S(2)}, u32[]{:S(2)}) async-start(bf16[8,32,128]{2,1,0:T(8,128)(2,1)} %select_select_fusion.2), calls=%async_computation.2 | async-start | bytes 131072 | tf_op jit(solution)/shard_map/all_to_all | solution.py:144
  46.8 23.1 %copy-start.17 = (pred[96]{0:T(512)(128)(4,1)}, pred[96]{0:T(512)(128)(4,1)S(1)}, u32[]{:S(2)}) copy-start(pred[96]{0:T(512)(128)(4,1)S(1)} %compare_and_fusion.3) | copy-start | bytes 292
  50.2 15.6 %all-to-all-start.1 = ((bf16[8,32,1024]{2,1,0:T(8,128)(2,1)}), bf16[8,32,1024]{2,1,0:T(8,128)(2,1)S(1)}, u32[]{:S(2)}, u32[]{:S(2)}) async-start(bf16[8,32,1024]{2,1,0:T(8,128)(2,1)} %select_select_fusion), calls=%async_computation.1 | async-start | bytes 1048576 | tf_op jit(solution)/shard_map/all_to_all | solution.py:143
  54.8 5.0 %copy-start.11 = (f32[1,128,128]{1,2,0:T(8,128)}, f32[1,128,128]{1,2,0:T(8,128)S(1)}, u32[]{:S(2)}) copy-start(f32[1,128,128]{1,2,0:T(8,128)S(1)} %convolution_bitcast_fusion.3) | copy-start | bytes 196612
  55.5 52.5 %collective-permute-start.2 = (f32[1,128,24]{1,2,0:T(8,128)}, f32[1,128,24]{1,2,0:T(8,128)}, u32[]{:S(2)}, u32[]{:S(2)}) collective-permute-start(f32[1,128,24]{1,2,0:T(8,128)} %get-tuple-element.31), channel_id=1, source_target_pairs={{0,2},{1,3},{4,6},{5,7},{8,10},{9,11},{12,14},{13,15},{16,18},{17,... | collective-permute-start | bytes 36872 | tf_op jit(solution)/shard_map/ppermute | solution.py:22
  59.9 48.1 %collective-permute-start.3 = (f32[1,128,24]{1,2,0:T(8,128)}, f32[1,128,24]{1,2,0:T(8,128)}, u32[]{:S(2)}, u32[]{:S(2)}) collective-permute-start(f32[1,128,24]{1,2,0:T(8,128)} %get-tuple-element.32), channel_id=1, source_target_pairs={{2,0},{3,1},{6,4},{7,5},{10,8},{11,9},{14,12},{15,13},{18,16},{19,... | collective-permute-start | bytes 36872 | tf_op jit(solution)/shard_map/ppermute | solution.py:24
  67.2 2.7 copy-start.4
  69.9 1.2 copy-start.20
  71.1 1.3 copy-start.2
  74.8 10.6 %all-to-all-start.3 = ((f32[8,1,2048]{2,1,0:T(1,128)}), f32[8,1,2048]{2,1,0:T(1,128)S(1)}, u32[]{:S(2)}, u32[]{:S(2)}) async-start(f32[8,1,2048]{2,1,0:T(1,128)} %reshape.575), calls=%async_computation.3 | async-start | bytes 131072 | tf_op jit(solution)/shard_map/all_to_all | solution.py:168
  78.4 186.1 %all-reduce.4.cloned.1.call-start = ((), (), s32[]{:S(2)}) async-start(), calls=%async_computation.4 | async-start | bytes 131072 | tf_op jit(solution)/shard_map/psum | solution.py:174
  78.5 9.2 %copy-start.8 = (pred[128,128]{1,0:T(8,128)(4,1)S(1)}, pred[128,128]{1,0:T(8,128)(4,1)}, u32[]{:S(2)}) copy-start(pred[128,128]{1,0:T(8,128)(4,1)} %broadcast_in_dim.160) | copy-start | bytes 49156
  78.5 9.2 %copy-start.9 = (pred[128,128]{1,0:T(8,128)(4,1)S(1)}, pred[128,128]{1,0:T(8,128)(4,1)}, u32[]{:S(2)}) copy-start(pred[128,128]{1,0:T(8,128)(4,1)} %broadcast_in_dim.162) | copy-start | bytes 49156
  78.5 29.5 %copy-start.12 = (f32[1,128,128]{1,2,0:T(8,128)S(1)}, f32[1,128,128]{1,2,0:T(8,128)}, u32[]{:S(2)}) copy-start(f32[1,128,128]{1,2,0:T(8,128)} %copy-done.11) | copy-start | bytes 196612
  78.5 33.9 %copy-start.18 = (pred[96]{0:T(512)(128)(4,1)S(1)}, pred[96]{0:T(512)(128)(4,1)}, u32[]{:S(2)}) copy-start(pred[96]{0:T(512)(128)(4,1)} %copy-done.17) | copy-start | bytes 292
  109.8 2.6 copy-start.15
  109.8 6.7 %collective-permute-start.4 = (f32[1,24,128]{2,1,0:T(8,128)S(1)}, f32[1,24,128]{2,1,0:T(8,128)S(1)}, u32[]{:S(2)}, u32[]{:S(2)}) collective-permute-start(f32[1,24,128]{2,1,0:T(8,128)S(1)} %get-tuple-element.28), channel_id=1, source_target_pairs={{0,4},{4,8},{8,12},{1,5},{5,9},{9,13},{2,6},{6,10},{10,14},{3,7},{... | collective-permute-start | bytes 36872 | tf_op jit(solution)/shard_map/ppermute | solution.py:22
  111.1 5.6 %collective-permute-start.5 = (f32[1,24,128]{2,1,0:T(8,128)S(1)}, f32[1,24,128]{2,1,0:T(8,128)S(1)}, u32[]{:S(2)}, u32[]{:S(2)}) collective-permute-start(f32[1,24,128]{2,1,0:T(8,128)S(1)} %get-tuple-element.29), channel_id=1, source_target_pairs={{4,0},{8,4},{12,8},{5,1},{9,5},{13,9},{6,2},{10,6},{14,10},{7,3},{... | collective-permute-start | bytes 36872 | tf_op jit(solution)/shard_map/ppermute | solution.py:24
  112.4 10.5 %copy-start.1 = (bf16[96,64,128]{2,1,0:T(8,128)(2,1)S(1)}, bf16[96,64,128]{2,1,0:T(8,128)(2,1)}, u32[]{:S(2)}) copy-start(bf16[96,64,128]{2,1,0:T(8,128)(2,1)} %multiply_convert_fusion.1) | copy-start | bytes 4718596
  116.5 10.7 %copy-start.7 = (bf16[1,128,128]{2,1,0:T(8,128)(2,1)S(1)}, bf16[1,128,128]{2,1,0:T(8,128)(2,1)}, u32[]{:S(2)}) copy-start(bf16[1,128,128]{2,1,0:T(8,128)(2,1)} %param.9) | copy-start | bytes 98308
  116.5 18.3 %copy-start.3 = (bf16[96,64,128]{2,1,0:T(8,128)(2,1)S(1)}, bf16[96,64,128]{2,1,0:T(8,128)(2,1)}, u32[]{:S(2)}) copy-start(bf16[96,64,128]{2,1,0:T(8,128)(2,1)} %copy-done.2) | copy-start | bytes 4718596
  118.7 8.5 %copy-start.14 = (f32[1,128,128]{1,2,0:T(8,128)}, f32[1,128,128]{1,2,0:T(8,128)S(1)}, u32[]{:S(2)}) copy-start(f32[1,128,128]{1,2,0:T(8,128)S(1)} %convolution_bitcast_fusion.2) | copy-start | bytes 196612
  118.7 7.5 %collective-permute-start.6 = (f32[1,128,24]{1,2,0:T(8,128)S(1)}, f32[1,128,24]{1,2,0:T(8,128)S(1)}, u32[]{:S(2)}, u32[]{:S(2)}) collective-permute-start(f32[1,128,24]{1,2,0:T(8,128)S(1)} %get-tuple-element.26), channel_id=1, source_target_pairs={{0,2},{1,3},{4,6},{5,7},{8,10},{9,11},{12,14},{13,15},{16,18},{17,... | collective-permute-start | bytes 36872 | tf_op jit(solution)/shard_map/ppermute | solution.py:22
  121.6 5.6 %collective-permute-start.7 = (f32[1,128,24]{1,2,0:T(8,128)S(1)}, f32[1,128,24]{1,2,0:T(8,128)S(1)}, u32[]{:S(2)}, u32[]{:S(2)}) collective-permute-start(f32[1,128,24]{1,2,0:T(8,128)S(1)} %get-tuple-element.27), channel_id=1, source_target_pairs={{2,0},{3,1},{6,4},{7,5},{10,8},{11,9},{14,12},{15,13},{18,16},{19,... | collective-permute-start | bytes 36872 | tf_op jit(solution)/shard_map/ppermute | solution.py:24
  129.1 37.2 %collective-permute-start.8 = (f32[1,24,128]{2,1,0:T(8,128)S(1)}, f32[1,24,128]{2,1,0:T(8,128)S(1)}, u32[]{:S(2)}, u32[]{:S(2)}) collective-permute-start(f32[1,24,128]{2,1,0:T(8,128)S(1)} %get-tuple-element.24), channel_id=1, source_target_pairs={{0,4},{4,8},{8,12},{1,5},{5,9},{9,13},{2,6},{6,10},{10,14},{3,7},{... | collective-permute-start | bytes 36872 | tf_op jit(solution)/shard_map/ppermute | solution.py:22
  133.6 32.7 %collective-permute-start.9 = (f32[1,24,128]{2,1,0:T(8,128)S(1)}, f32[1,24,128]{2,1,0:T(8,128)S(1)}, u32[]{:S(2)}, u32[]{:S(2)}) collective-permute-start(f32[1,24,128]{2,1,0:T(8,128)S(1)} %get-tuple-element.25), channel_id=1, source_target_pairs={{4,0},{8,4},{12,8},{5,1},{9,5},{13,9},{6,2},{10,6},{14,10},{7,3},{... | collective-permute-start | bytes 36872 | tf_op jit(solution)/shard_map/ppermute | solution.py:24
  167.4 3.8 %collective-permute-start.10 = (f32[1,128,24]{1,2,0:T(8,128)S(1)}, f32[1,128,24]{1,2,0:T(8,128)S(1)}, u32[]{:S(2)}, u32[]{:S(2)}) collective-permute-start(f32[1,128,24]{1,2,0:T(8,128)S(1)} %get-tuple-element.22), channel_id=1, source_target_pairs={{0,2},{1,3},{4,6},{5,7},{8,10},{9,11},{12,14},{13,15},{16,18},{17,... | collective-permute-start | bytes 36872 | tf_op jit(solution)/shard_map/ppermute | solution.py:22
  168.7 5.6 %collective-permute-start.11 = (f32[1,128,24]{1,2,0:T(8,128)S(1)}, f32[1,128,24]{1,2,0:T(8,128)S(1)}, u32[]{:S(2)}, u32[]{:S(2)}) collective-permute-start(f32[1,128,24]{1,2,0:T(8,128)S(1)} %get-tuple-element.23), channel_id=1, source_target_pairs={{2,0},{3,1},{6,4},{7,5},{10,8},{11,9},{14,12},{15,13},{18,16},{19,... | collective-permute-start | bytes 36872 | tf_op jit(solution)/shard_map/ppermute | solution.py:24
  175.3 92.9 %copy-start.13 = (f32[1,128,128]{2,1,0:T(8,128)}, f32[1,128,128]{2,1,0:T(8,128)S(1)}, u32[]{:S(2)}) copy-start(f32[1,128,128]{2,1,0:T(8,128)S(1)} %fusion.3) | copy-start | bytes 196612
  175.4 3.7 %collective-permute-start.12 = (f32[1,24,128]{2,1,0:T(8,128)S(1)}, f32[1,24,128]{2,1,0:T(8,128)S(1)}, u32[]{:S(2)}, u32[]{:S(2)}) collective-permute-start(f32[1,24,128]{2,1,0:T(8,128)S(1)} %get-tuple-element.20), channel_id=1, source_target_pairs={{0,4},{4,8},{8,12},{1,5},{5,9},{9,13},{2,6},{6,10},{10,14},{3,7},{... | collective-permute-start | bytes 36872 | tf_op jit(solution)/shard_map/ppermute | solution.py:22
  176.7 5.6 %collective-permute-start.13 = (f32[1,24,128]{2,1,0:T(8,128)S(1)}, f32[1,24,128]{2,1,0:T(8,128)S(1)}, u32[]{:S(2)}, u32[]{:S(2)}) collective-permute-start(f32[1,24,128]{2,1,0:T(8,128)S(1)} %get-tuple-element.21), channel_id=1, source_target_pairs={{4,0},{8,4},{12,8},{5,1},{9,5},{13,9},{6,2},{10,6},{14,10},{7,3},{... | collective-permute-start | bytes 36872 | tf_op jit(solution)/shard_map/ppermute | solution.py:24
  183.3 83.2 %collective-permute-start.14 = (f32[1,128,24]{1,2,0:T(8,128)S(1)}, f32[1,128,24]{1,2,0:T(8,128)S(1)}, u32[]{:S(2)}, u32[]{:S(2)}) collective-permute-start(f32[1,128,24]{1,2,0:T(8,128)S(1)} %get-tuple-element.18), channel_id=1, source_target_pairs={{0,2},{1,3},{4,6},{5,7},{8,10},{9,11},{12,14},{13,15},{16,18},{17,... | collective-permute-start | bytes 36872 | tf_op jit(solution)/shard_map/ppermute | solution.py:22
  185.0 81.5 %collective-permute-start.15 = (f32[1,128,24]{1,2,0:T(8,128)S(1)}, f32[1,128,24]{1,2,0:T(8,128)S(1)}, u32[]{:S(2)}, u32[]{:S(2)}) collective-permute-start(f32[1,128,24]{1,2,0:T(8,128)S(1)} %get-tuple-element.19), channel_id=1, source_target_pairs={{2,0},{3,1},{6,4},{7,5},{10,8},{11,9},{14,12},{15,13},{18,16},{19,... | collective-permute-start | bytes 36872 | tf_op jit(solution)/shard_map/ppermute | solution.py:24
Sparse Core Ops, SparseCore 0:
  179.2 85.2 all-reduce.3
where the time goes:
time: 277 us; the launch traced here: 275 us
  waiting for transfers between devices  96.3 us (35%)
  starting transfers between devices  52.5 us (19%)
  blocking collectives  50 us (18%)
  matrix products  23.8 us (9%)
  other arithmetic  18.9 us (7%)
  local copies, waits for them, and re-layouts  17.4 us (6%)
  between operations  16.1 us (6%)
    psum x1, waiting for transfers between devices, local(): lax.psum((grads[0], grads[1], grads[2], weight_part), ('rows', 'cols', 'm...  78.2 us
    psum x1, blocking collectives, local(): lax.psum((grads[0], grads[1], grads[2], weight_part), ('rows', 'cols', 'm...  31.1 us
    ppermute x8, starting transfers between devices, extended(): lax.ppermute(tail, axis, [(i, (i + 1) % count) for i in range(ends)])  22.1 us
    psum x1, blocking collectives, local(): lax.psum((jnp.sum(source, axis=(1, 2)), jnp.sum(target, axis=(1, 2))), ('...  19 us
    ppermute x8, starting transfers between devices, extended(): lax.ppermute(head, axis, [((i + 1) % count, i) for i in range(ends)])  10.3 us
    ppermute x8, waiting for transfers between devices, extended(): lax.ppermute(head, axis, [((i + 1) % count, i) for i in range(ends)])  7.46 us
    all_to_all x1, starting transfers between devices, local(): lax.all_to_all(sent_flags, ('rows', 'cols'), split_axis=0, concat_axis=0,...  6.87 us
    dot_general x4, matrix products, smooth(): result = jnp.einsum('mij,cj->mic', widened, band_cols, precision=HIGHEST)  6.48 us
  transfers between devices with their start and end apart: 21, of which 8 were waited for; matrix products, arithmetic and copies ran while one was open for 18% of the time, Pallas kernels for 0%

commit v1 on v0

v1 whole, which is shorter than its diff:
```python
import functools

import jax
import jax.numpy as jnp
import ml_dtypes
import numpy as np
from jax import lax
from jax.experimental import pallas as pl
from jax.experimental.pallas import tpu as pltpu
from jax.sharding import PartitionSpec as P

RADIUS = 24
F32 = jnp.float32
BF = jnp.bfloat16


def net_kernel(drv, obs, conf, mask, w1, w2, wo, g_out, src_out, tgt_out, left_out, right_out):
    rows = mask.shape[0]
    hid = w2.shape[0]
    feat = w1.shape[0]
    w1h = (w1[...].astype(F32) * 0.5).T.astype(BF)
    w2f = w2[...].astype(F32)
    w2h = (w2f * 0.5).T.astype(BF)
    w2b = w2[...]
    wo_row = wo[...].astype(F32)
    wo_col = jnp.broadcast_to(wo_row * 0.5, (128, hid)).T
    wo8 = jnp.broadcast_to(wo_row, (8, hid)).astype(BF)
    sub = lax.broadcasted_iota(jnp.int32, (8, 128), 0)

    def body(i, carry):
        second, first, outg, wsum, ssum, tsum = carry
        r0 = pl.multiple_of(i * 16, 16)
        x3 = jnp.swapaxes(drv[0, :, pl.ds(r0, 16), :].astype(F32), 0, 1).astype(BF)
        ob = obs[0, pl.ds(r0, 16), :].astype(F32)
        cf = conf[0, pl.ds(r0, 16), :].astype(F32)
        mk = mask[pl.ds(r0, 16), :].astype(F32)
        wm = (cf * mk).astype(BF).astype(F32)
        tg = ob * mk + 0.1
        tgt_out[pl.ds(r0, 16), :] = tg
        wsum += wm[:8] + wm[8:]
        tsum += tg[:8] + tg[8:]
        for half in range(2):
            x = jnp.concatenate([x3[half * 8 + r] for r in range(8)], axis=1)
            p1 = jnp.dot(w1h, x, preferred_element_type=F32)
            t1 = jnp.tanh(p1)
            u1 = 1.0 + t1
            h1 = (p1 * u1).astype(BF)
            s1 = u1 * (0.5 + (0.5 * p1) * (1.0 - t1))
            p2 = jnp.dot(w2h, h1, preferred_element_type=F32)
            t2 = jnp.tanh(p2)
            u2 = 1.0 + t2
            h2 = (p2 * u2).astype(BF)
            sc8 = jnp.dot(wo8, h2, preferred_element_type=F32)
            score = sc8[:, 0:128]
            for r in range(1, 8):
                score = jnp.where(sub == r, sc8[:, r * 128:(r + 1) * 128], score)
            e = jnp.exp(-jnp.abs(score))
            imitated = jnp.maximum(score, 0.0) + jnp.log1p(e)
            sig = jnp.where(score >= 0, 1.0, e) / (1.0 + e)
            sl = slice(half * 8, half * 8 + 8)
            delta = wm[sl] * (imitated - ob[sl]) * sig
            sr = mk[sl] * imitated + 0.1
            src_out[pl.ds(r0 + half * 8, 8), :] = sr
            ssum += sr
            drow = jnp.concatenate([jnp.broadcast_to(delta[r:r + 1], (8, 128)) for r in range(8)], axis=1)
            dhi = drow.astype(BF)
            dlo = (drow - dhi.astype(F32)).astype(BF)
            sub1 = lax.broadcasted_iota(jnp.int32, (8, 1024), 0)
            dmix = jnp.where(sub1 == 0, dhi.astype(F32), dlo.astype(F32)).astype(BF)
            dw = jnp.concatenate([
                wo_col * jnp.concatenate([drow[:, r * 128:(r + 1) * 128]] * 16, axis=0) for r in range(8)], axis=1)
            d2 = (dw * (u2 * (1.0 + p2 * (1.0 - t2)))).astype(BF)
            nt = (((1,), (1,)), ((), ()))
            second += lax.dot_general(h1, d2, nt, preferred_element_type=F32)
            outg += lax.dot_general(dmix, h2, nt, preferred_element_type=F32)
            back = jnp.dot(w2b, d2, preferred_element_type=F32)
            d1 = (back * s1).astype(BF)
            first += lax.dot_general(x, d1, nt, preferred_element_type=F32)
        return second, first, outg, wsum, ssum, tsum

    z8 = jnp.zeros((8, 128), F32)
    second, first, outg, wsum, ssum, tsum = lax.fori_loop(
        0, rows // 16, body,
        (jnp.zeros((hid, hid), F32), jnp.zeros((feat, hid), F32), z8, z8, z8, z8))
    g_out[0:hid, :] = second
    g_out[hid:hid + feat, :] = first
    og = outg[0:1] + outg[1:2]
    lane = lax.broadcasted_iota(jnp.int32, (8, 128), 1)
    me = lax.axis_index("maps")
    tot = lambda v: jnp.sum(jnp.sum(v, axis=1, keepdims=True), axis=0, keepdims=True)
    extra = jnp.where(sub == 0, og, 0.0)
    extra = jnp.where(sub == 1, tot(wsum), extra)
    extra = jnp.where(sub == 2 + me, tot(ssum), extra)
    extra = jnp.where(sub == 4 + me, tot(tsum), extra)
    g_out[hid + feat:hid + feat + 8, :] = extra
    lanes = lax.broadcasted_iota(jnp.int32, (rows, 128), 1)
    left, right = edge_strips(src_out[...], tgt_out[...], lanes)
    left_out[...] = left
    if lax.axis_size("cols") == 2:
        right = jnp.where(lax.axis_index("cols") == 0, right, left)
    right_out[...] = right

def net(drivers, observed, confidence, land_mask, w1, w2, wo):
    feat, hid = w1.shape
    R, C = land_mask.shape
    return pl.pallas_call(
        net_kernel,
        out_shape=(jax.ShapeDtypeStruct((hid + feat + 8, 128), F32),
                   *[jax.ShapeDtypeStruct((R, C), F32)] * 4),
        name="net",
    )(drivers, observed, confidence, land_mask, w1, w2, wo.reshape(1, hid))


def edge_strips(src, tgt, lane):
    right = jnp.where(lane >= 128 - 3 * RADIUS, src, pltpu.roll(tgt, 2 * RADIUS, 1))
    left = jnp.where(lane < 3 * RADIUS, src, pltpu.roll(tgt, 128 - 2 * RADIUS, 1))
    return left, right


def left_block(strip, lane):
    src = jnp.where(lane >= 128 - 3 * RADIUS, strip, 0.0)
    tgt = jnp.where(lane >= 128 - 2 * RADIUS, pltpu.roll(strip, 128 - 2 * RADIUS, 1), 0.0)
    return src, tgt


def right_block(strip, lane):
    src = jnp.where(lane < 3 * RADIUS, strip, 0.0)
    tgt = jnp.where(lane < 2 * RADIUS, pltpu.roll(strip, 2 * RADIUS, 1), 0.0)
    return src, tgt


def widen(src, tgt, strips):
    lane = lax.broadcasted_iota(jnp.int32, src.shape, 1)
    if not strips:
        return src, tgt
    if len(strips) == 1:
        at_left = lax.axis_index("cols") == 0
        rs, rt = right_block(strips[0], lane)
        ls, lt = left_block(strips[0], lane)
        wide_src = jnp.concatenate([jnp.where(at_left, src, ls), jnp.where(at_left, rs, src)], axis=1)
        wide_tgt = jnp.concatenate([jnp.where(at_left, tgt, lt), jnp.where(at_left, rt, tgt)], axis=1)
        return wide_src, wide_tgt
    ls, lt = left_block(strips[0], lane)
    rs, rt = right_block(strips[1], lane)
    return jnp.concatenate([ls, src, rs], axis=1), jnp.concatenate([lt, tgt, rt], axis=1)


def halo_kernel(src_ref, tgt_ref, *refs):
    strips = [ref[...] for ref in refs[:-2]]
    up_ref, down_ref = refs[-2:]
    src, tgt = widen(src_ref[...], tgt_ref[...], strips)
    far, near = 3 * RADIUS, 2 * RADIUS
    rows = src.shape[0]
    up_ref[0:far, :] = src[0:far]
    up_ref[far:far + near, :] = tgt[0:near]
    down_ref[0:far, :] = src[rows - far:rows]
    down_ref[far:far + near, :] = tgt[rows - near:rows]


def halo(src, tgt, strips):
    width = src.shape[1] * (1 + len(strips))
    shape = jax.ShapeDtypeStruct((5 * RADIUS, width), F32)
    return pl.pallas_call(halo_kernel, out_shape=(shape, shape), name="halo")(src, tgt, *strips)


def parts(value):
    high = value.astype(BF)
    return high, (value - high.astype(F32)).astype(BF)


def product(left, right):
    (lh, ll), (rh, rl) = left, right
    dot = functools.partial(jnp.dot, preferred_element_type=F32)
    return dot(lh, rh) + (dot(lh, rl) + dot(ll, rh))


def sinkhorn_kernel(first_last, src_ref, tgt_ref, above_ref, below_ref, brow_ref, bcol_ref, krow_ref, kcol_ref, *refs):
    strips = [ref[...] for ref in refs[:-2]]
    source_out, target_out = refs[-2:]
    far, near = 3 * RADIUS, 2 * RADIUS
    rows = src_ref.shape[0]
    wide = above_ref.shape[1]
    src, tgt = widen(src_ref[...], tgt_ref[...], strips)
    source = jnp.concatenate([above_ref[0:far, :], src, below_ref[0:far, :]], axis=0)
    target = jnp.concatenate([above_ref[far:far + near, :], tgt, below_ref[far:far + near, :]], axis=0)
    rows_at, cols_at = lax.axis_index("rows"), lax.axis_index("cols")
    row_first = (rows_at == 0).astype(F32)
    row_last = (rows_at == lax.axis_size("rows") - 1).astype(F32)
    krow = 1.0 - row_first * krow_ref[0] - row_last * krow_ref[1]
    if len(strips) == 2:
        col_first = (cols_at == 0).astype(F32)
        col_last = (cols_at == lax.axis_size("cols") - 1).astype(F32)
        kcol = 1.0 - col_first * kcol_ref[0:1, :] - col_last * kcol_ref[1:2, :]
        own = 128
    else:
        kcol = 1.0 - kcol_ref[0:1, :] - kcol_ref[1:2, :]
        own = pl.multiple_of(cols_at * 128, 128) if strips else 0
    krow = jnp.concatenate([krow] * (wide // 128), axis=1)
    brow = (brow_ref[0], brow_ref[1])
    bcol = (bcol_ref[0], bcol_ref[1])

    def smooth(field, count, columns):
        bands = tuple(band[0:count, 0:count + near] for band in brow)
        return product(parts(product(bands, parts(field))), columns)

    def ratio(top, bottom):
        inside = top > 0.0
        return jnp.where(inside, top / jnp.where(inside, bottom, 1.0), 0.0)

    scaling = source / (krow * kcol)
    scaling = ratio(target, smooth(scaling, rows + 2 * near, bcol))
    scaling = ratio(source[near:near + rows + near], smooth(scaling, rows + near, bcol))
    bottom = smooth(scaling, rows, tuple(bcol_ref[i, :, pl.ds(own, 128)] for i in range(2)))
    if len(strips) == 1:
        source_out[...] = jnp.where(cols_at == 0, scaling[RADIUS:RADIUS + rows, 0:128], scaling[RADIUS:RADIUS + rows, 128:256])
    else:
        source_out[...] = scaling[RADIUS:RADIUS + rows, own:own + 128]
    target_out[...] = tgt_ref[...] / bottom


def split_table(table):
    high = table.astype(ml_dtypes.bfloat16)
    low = (table - high.astype(np.float64)).astype(ml_dtypes.bfloat16)
    return np.stack([high, low])


def taps():
    offsets = np.arange(-RADIUS, RADIUS + 1, dtype=np.float64)
    weights = np.exp(-4.5 * offsets * offsets / (RADIUS * RADIUS))
    return weights / weights.sum()


def tails(start, count, end):
    weights = taps()
    before, after = np.zeros(count), np.zeros(count)
    for at in range(count):
        if at >= start:
            before[at] = weights[: max(0, RADIUS - (at - start))].sum()
        if at < end:
            after[at] = weights[: max(0, RADIUS - (end - 1 - at))].sum()
    return np.stack([before, after])


def sinkhorn(src, tgt, above, below, strips):
    rows, cols = src.shape
    wide = above.shape[1]
    weights = taps()

    def toeplitz(count_out, count_in, shift):
        offset = np.arange(count_in)[None, :] - np.arange(count_out)[:, None] + shift
        inside = (offset >= 0) & (offset <= 2 * RADIUS)
        return np.where(inside, weights[np.clip(offset, 0, 2 * RADIUS)], 0.0)

    brow = split_table(toeplitz(rows + 4 * RADIUS, rows + 6 * RADIUS, 0))
    bcol = split_table(toeplitz(wide, wide, RADIUS))
    krow = tails(3 * RADIUS, rows + 6 * RADIUS, 3 * RADIUS + rows)
    krow = np.broadcast_to(krow[:, :, None], krow.shape + (128,)).astype(np.float32)
    if len(strips) == 2:
        kcol = tails(cols, wide, 2 * cols)
    else:
        kcol = tails(0, wide, wide)
    kcol = np.concatenate([kcol, np.zeros((6, wide))]).astype(np.float32)
    shape = jax.ShapeDtypeStruct((rows, cols), F32)
    return pl.pallas_call(functools.partial(sinkhorn_kernel, None), out_shape=(shape, shape), name="sinkhorn")(
        src, tgt, above, below, jnp.asarray(brow), jnp.asarray(bcol), jnp.asarray(krow), jnp.asarray(kcol), *strips
    )


def finish_kernel(cells, hid, feat, *refs):
    count = len(refs) - 7
    sums = refs[0][...]
    for ref in refs[1:count]:
        sums = sums + ref[...]
    source_ref, target_ref = refs[count:count + 2]
    first_out, second_out, output_out, source_out, target_out = refs[count + 2:]
    tail = sums[hid + feat:hid + feat + 8]
    me = lax.axis_index("maps")
    maps = lax.axis_size("maps")
    inverse = 1.0 / tail[1:2]
    second_out[...] = sums[0:hid] * inverse
    first_out[...] = sums[hid:hid + feat] * inverse
    output_out[...] = tail[0:1] * inverse
    source_mean, target_mean = tail[2:3], tail[2 + maps:3 + maps]
    for other in range(1, maps):
        source_mean = jnp.where(me == other, tail[2 + other:3 + other], source_mean)
        target_mean = jnp.where(me == other, tail[2 + maps + other:3 + maps + other], target_mean)
    source_mean, target_mean = source_mean * (1.0 / cells), target_mean * (1.0 / cells)
    ratio = source_mean / target_mean
    source_out[0] = source_ref[...] * (1.0 / (source_mean * ratio))
    target_out[0] = target_ref[...] * (ratio * ratio)


def finish(sums, source, target, cells, hid, feat):
    shape = jax.ShapeDtypeStruct((1,) + source.shape, F32)
    return pl.pallas_call(
        functools.partial(finish_kernel, cells, hid, feat),
        out_shape=(
            jax.ShapeDtypeStruct((feat, hid), F32),
            jax.ShapeDtypeStruct((hid, hid), F32),
            jax.ShapeDtypeStruct((1, hid), F32),
            shape,
            shape,
        ),
        name="finish",
    )(*sums, source, target)


def swap(value, axis, step):
    return lax.ppermute(value, axis, [(i, i ^ step) for i in range(lax.axis_size(axis))])


def local(
    drivers, observed, confidence, land_mask, ownership, first_layer, second_layer, output_layer
):
    feat, hid = first_layer.shape
    row_count, col_count = lax.axis_size("rows"), lax.axis_size("cols")
    cells = land_mask.size * row_count * col_count
    sums, src, tgt, left, right = net(
        drivers, observed, confidence, land_mask, first_layer, second_layer, output_layer
    )
    if col_count == 1:
        strips = []
    elif col_count == 2:
        strips = [swap(right, "cols", 1)]
    else:
        strips = [
            lax.ppermute(right, "cols", [(i, i + 1) for i in range(col_count - 1)]),
            lax.ppermute(left, "cols", [(i + 1, i) for i in range(col_count - 1)]),
        ]
    up, down = halo(src, tgt, strips)
    above = lax.ppermute(down, "rows", [(i, i + 1) for i in range(row_count - 1)])
    below = lax.ppermute(up, "rows", [(i + 1, i) for i in range(row_count - 1)])
    source, target = sinkhorn(src, tgt, above, below, strips)
    steps = []
    for axis in ("maps", "cols", "rows"):
        step = 1
        while step < lax.axis_size(axis):
            steps.append((axis, step))
            step *= 2
    pending = [sums]
    for axis, step in steps:
        total = pending[0] if len(pending) == 1 else pending[0] + pending[1]
        pending = [total, swap(total, axis, step)]
    first, second, output, source, target = finish(pending, source, target, cells, hid, feat)
    return first, second, output.reshape(hid), source, target


def solution(mesh):
    in_specs = (
        P(("groups", "maps"), None, "rows", "cols"),
        P(("groups", "maps"), "rows", "cols"),
        P(("groups", "maps"), "rows", "cols"),
        P(("groups", "rows"), "cols"),
        P(("groups", "rows"), "cols"),
        P(),
        P(),
        P(),
    )
    out_specs = (
        P("groups", None),
        P("groups", None),
        P("groups"),
        P(("groups", "maps"), "rows", "cols"),
        P(("groups", "maps"), "rows", "cols"),
    )
    return jax.shard_map(local, mesh=mesh, in_specs=in_specs, out_specs=out_specs, check_vma=False)
```

time: 277 us -> 48.9 us (0.18)
  waiting for transfers between devices: 96.3 us -> 6.26 us
  blocking collectives: 50 us -> 0 us
  starting transfers between devices: 52.5 us -> 14.1 us
  Pallas kernels: 0 us -> 24.6 us
  matrix products: 23.8 us -> 0 us
  other arithmetic: 18.9 us -> 0.92 us
  local copies, waits for them, and re-layouts: 17.4 us -> 1.91 us
  between operations: 16.1 us -> 0.7 us
    psum x1 -> x0, waiting for transfers between devices: 78.2 us -> none  [local(): lax.psum((grads[0], grads[1], grads[2], weight_part), ('rows', 'cols', 'm...]
    psum x2 -> x0, blocking collectives: 50 us -> none  [the longest x1 31.1 us: local(): lax.psum((grads[0], grads[1], grads[2], weight_part), ('rows', 'cols', 'm...]
    pallas_call x0 -> x4, Pallas kernels: none -> 24.6 us  [the longest x1 17.6 us: net(): pl.pallas_call(net_kernel, out_shape=(jax.ShapeDtypeStruct((hid + feat +...]
    dot_general x14 -> x0, matrix products: 23.8 us -> none  [the longest x4 6.48 us: smooth(): result = jnp.einsum('mij,cj->mic', widened, band_cols, precision=HIGHEST)]
    all_to_all x4 -> x0, starting transfers between devices: 20 us -> none  [the longest x1 6.87 us: local(): lax.all_to_all(sent_flags, ('rows', 'cols'), split_axis=0, concat_axis=0,...]
    ppermute x16 -> x7, starting transfers between devices: 32.5 us -> 14.1 us  [the longest x5 10.2 us: swap(): lax.ppermute(value, axis, [(i, i ^ step) for i in range(lax.axis_size(axi...]
    all_to_all x4 -> x0, waiting for transfers between devices: 10.6 us -> none  [the longest x1 3.63 us: local(): lax.all_to_all(returned, ('rows', 'cols'), split_axis=0, concat_axis=0, t...]
    gather x9 -> x0, local copies, waits for them, and re-layouts: 5.64 us -> none  [the longest x2 1.56 us: local(): jnp.take(blocks, source_block, axis=0)]
  transfers between devices with their start and end apart: 21 -> 7, of which waited for: 8 -> 3; matrix products, arithmetic and copies ran while one was open for 18% -> 0% of each run, Pallas kernels for 0% -> 11%
where the time goes in v1:
time: 48.9 us; the launch traced here: 48.5 us
  Pallas kernels  24.6 us (50%)
  starting transfers between devices  14.1 us (29%)
  waiting for transfers between devices  6.26 us (13%)
  local copies, waits for them, and re-layouts  1.91 us (4%)
  other arithmetic  0.92 us (2%)
  between operations  0.7 us (1%)
    pallas_call x1, Pallas kernels, net(): pl.pallas_call(net_kernel, out_shape=(jax.ShapeDtypeStruct((hid + feat +...  17.6 us
    ppermute x5, starting transfers between devices, swap(): lax.ppermute(value, axis, [(i, i ^ step) for i in range(lax.axis_size(axi...  10.2 us
    ppermute x5, waiting for transfers between devices, swap(): lax.ppermute(value, axis, [(i, i ^ step) for i in range(lax.axis_size(axi...  3.94 us
    pallas_call x1, Pallas kernels, sinkhorn(): pl.pallas_call(functools.partial(sinkhorn_kernel, None), out_shape=(shape...  3.63 us
    ppermute x1, starting transfers between devices, local(): lax.ppermute(down, 'rows', [(i, i + 1) for i in range(row_count - 1)])  2.69 us
    ppermute x1, waiting for transfers between devices, local(): below = lax.ppermute(up, 'rows', [(i + 1, i) for i in range(row_count - 1)])  2.31 us
    unnamed x12, local copies, waits for them, and re-layouts  1.91 us
    pallas_call x1, Pallas kernels, halo(): pl.pallas_call(halo_kernel, out_shape=(shape, shape), name='halo')  1.68 us
  transfers between devices with their start and end apart: 7, of which 3 were waited for; matrix products, arithmetic and copies ran while one was open for 0% of the time, Pallas kernels for 11%

profile of v1, /device:TPU:0, one launch (start us, length us, event | category | flops | bytes accessed | tf_op | source)
XLA Modules:
  0.0 48.5 jit_solution(12168893335516622071)
XLA Ops:
  0.6 17.6 %net.1 = (f32[152,128]{1,0:T(8,128)}, f32[128,128]{1,0:T(8,128)}, f32[128,128]{1,0:T(8,128)}, f32[128,128]{1,0:T(8,128)}, f32[128,128]{1,0:T(8,128)}) custom-call(bf16[1,16,128,128]{3,2,1,0:T(8,128)(2,1)} %drv.1, bf16[1,128,128]{2,1,0:T(8,128)(2,1)} %obs.1, bf16[1,128,128]{2,1,0:T(8,128)(2,1)} %conf.1, s32[128,128]{1,0:T(8,128)} %mask.1, ...), custom_call_target="tpu_custom_call" | custom-call | tf_op jit(solution)/shard_map/net/pallas_call | solution.py:106
  18.3 0.0 copy-start.5
  18.3 0.4 collective-permute-start
  18.7 1.1 %collective-permute-done = f32[152,128]{1,0:T(8,128)S(1)} collective-permute-done((f32[152,128]{1,0:T(8,128)}, f32[152,128]{1,0:T(8,128)S(1)}, u32[]{:S(2)}, u32[]{:S(2)}) %collective-permute-start) | collective-permute-done | bytes 77856 | tf_op jit(solution)/shard_map/ppermute | solution.py:309
  19.8 0.9 %add.9 = f32[152,128]{1,0:T(8,128)S(1)} add(f32[152,128]{1,0:T(8,128)} %get-tuple-element.18, f32[152,128]{1,0:T(8,128)S(1)} %collective-permute-done) | non-fusion elementwise | flops 19456 | bytes 233472 | tf_op jit(solution)/shard_map/add | solution.py:342
  20.7 2.9 %collective-permute-start.1 = (f32[152,128]{1,0:T(8,128)S(1)}, f32[152,128]{1,0:T(8,128)S(1)}, u32[]{:S(2)}, u32[]{:S(2)}) collective-permute-start(f32[152,128]{1,0:T(8,128)S(1)} %add.9), channel_id=1, source_target_pairs={{0,2},{2,0},{1,3},{3,1},{4,6},{6,4},{5,7},{7,5},{8,10},{10,8},{9,1... | collective-permute-start | bytes 233480 | tf_op jit(solution)/shard_map/ppermute | solution.py:309
  23.7 0.0 copy-done.5
  23.7 0.1 collective-permute-start.4
  23.7 2.8 %collective-permute-done.1 = f32[152,128]{1,0:T(8,128)S(1)} collective-permute-done((f32[152,128]{1,0:T(8,128)S(1)}, f32[152,128]{1,0:T(8,128)S(1)}, u32[]{:S(2)}, u32[]{:S(2)}) %collective-permute-start.1) | collective-permute-done | bytes 77856 | tf_op jit(solution)/shard_map/ppermute | solution.py:309
  26.6 2.2 %collective-permute-start.2 = (f32[152,128]{1,0:T(8,128)S(1)}, f32[152,128]{1,0:T(8,128)S(1)}, u32[]{:S(2)}, u32[]{:S(2)}) collective-permute-start(f32[152,128]{1,0:T(8,128)S(1)} %add.10), channel_id=1, source_target_pairs={{0,4},{4,0},{8,12},{12,8},{1,5},{5,1},{9,13},{13,9},{2,6},{6,2},{1... | collective-permute-start | bytes 233480 | tf_op jit(solution)/shard_map/ppermute | solution.py:309
  28.8 0.0 collective-permute-done.4.refs_0_
  28.8 0.0 copy-start.1
  28.8 0.6 %copy-done.1 = f32[128,128]{1,0:T(8,128)} copy-done((f32[128,128]{1,0:T(8,128)}, f32[128,128]{1,0:T(8,128)S(1)}, u32[]{:S(2)}) %copy-start.1) | copy-done | bytes 65560
  29.4 1.7 %halo.1 = (f32[120,256]{1,0:T(8,128)}, f32[120,256]{1,0:T(8,128)}) custom-call(f32[128,128]{1,0:T(8,128)} %get-tuple-element.19.src_ref, f32[128,128]{1,0:T(8,128)} %get-tuple-element.20.tgt_ref, f32[128,128]{1,0:T(8,128)} %copy-done.1), custom_call_target="tpu_custom_call" | custom-call | tf_op jit(solution)/shard_map/halo/pallas_call | solution.py:163
  31.1 2.7 %collective-permute-start.5 = (f32[120,256]{1,0:T(8,128)}, f32[120,256]{1,0:T(8,128)S(1)}, u32[]{:S(2)}, u32[]{:S(2)}) collective-permute-start(f32[120,256]{1,0:T(8,128)} %get-tuple-element.22), channel_id=1, source_target_pairs={{0,4},{4,8},{8,12},{1,5},{5,9},{9,13},{2,6},{6,10},{10,14},{3,7},{... | collective-permute-start | bytes 368648 | tf_op jit(solution)/shard_map/ppermute | solution.py:331
  33.8 1.3 %collective-permute-start.6 = (f32[120,256]{1,0:T(8,128)}, f32[120,256]{1,0:T(8,128)S(1)}, u32[]{:S(2)}, u32[]{:S(2)}) collective-permute-start(f32[120,256]{1,0:T(8,128)} %get-tuple-element.23), channel_id=1, source_target_pairs={{4,0},{8,4},{12,8},{5,1},{9,5},{13,9},{6,2},{10,6},{14,10},{7,3},{... | collective-permute-start | bytes 368648 | tf_op jit(solution)/shard_map/ppermute | solution.py:332
  35.1 0.0 collective-permute-done.2
  35.1 0.0 copy-start
  35.1 4.5 %collective-permute-start.3 = (f32[152,128]{1,0:T(8,128)S(1)}, f32[152,128]{1,0:T(8,128)S(1)}, u32[]{:S(2)}, u32[]{:S(2)}) collective-permute-start(f32[152,128]{1,0:T(8,128)S(1)} %add.11.refs_0_), channel_id=1, source_target_pairs={{0,8},{4,12},{8,0},{12,4},{1,9},{5,13},{9,1},{13,5},{2,10},{6,14},... | collective-permute-start | bytes 233480 | tf_op jit(solution)/shard_map/ppermute | solution.py:309
  39.6 0.0 collective-permute-done.5.above_ref
  39.6 0.0 copy-start.2
  39.6 2.3 %collective-permute-done.6.below_ref = f32[120,256]{1,0:T(8,128)S(1)} collective-permute-done((f32[120,256]{1,0:T(8,128)}, f32[120,256]{1,0:T(8,128)S(1)}, u32[]{:S(2)}, u32[]{:S(2)}) %collective-permute-start.6) | collective-permute-done | bytes 122912 | tf_op jit(solution)/shard_map/ppermute | solution.py:332
  42.0 0.0 copy-done.2
  42.0 0.0 copy-start.3
  42.0 0.6 %copy-done.3 = f32[120,256]{1,0:T(8,128)} copy-done((f32[120,256]{1,0:T(8,128)}, f32[120,256]{1,0:T(8,128)S(1)}, u32[]{:S(2)}) %copy-start.3) | copy-done | bytes 122904
  42.6 3.6 %sinkhorn.1 = (f32[128,128]{1,0:T(8,128)}, f32[128,128]{1,0:T(8,128)}) custom-call(f32[128,128]{1,0:T(8,128)} %get-tuple-element.19.src_ref, f32[128,128]{1,0:T(8,128)} %get-tuple-element.20.tgt_ref, f32[120,256]{1,0:T(8,128)} %copy-done.2, f32[120,256]{1,0:T(8,128)} %copy-done.3, bf16[2,224,272]{2,1,0:T(8,128)(2,1)} %constant.8.clone.brow_ref, ...), custom_call_target="tpu_custom_call" | custom-call | tf_op jit(solution)/shard_map/sinkhorn/pallas_call | solution.py:264
  46.2 0.0 copy-done
  46.2 0.0 collective-permute-done.3.refs_1_
  46.2 0.0 copy-start.4
  46.3 0.6 %copy-done.4 = f32[152,128]{1,0:T(8,128)} copy-done((f32[152,128]{1,0:T(8,128)}, f32[152,128]{1,0:T(8,128)S(1)}, u32[]{:S(2)}) %copy-start.4) | copy-done | bytes 77848
  46.9 1.6 %finish.1 = (f32[16,128]{1,0:T(8,128)}, f32[128,128]{1,0:T(8,128)}, f32[1,128]{1,0:T(1,128)}, f32[1,128,128]{2,1,0:T(8,128)}, f32[1,128,128]{2,1,0:T(8,128)}) custom-call(f32[152,128]{1,0:T(8,128)} %copy-done, f32[152,128]{1,0:T(8,128)} %copy-done.4, f32[128,128]{1,0:T(8,128)} %get-tuple-element.24.refs_2_, f32[128,128]{1,0:T(8,128)} %get-tuple-element.25.refs_3_), custom_call_target="tpu_custom_call" | custom-call | tf_op jit(solution)/shard_map/finish/pallas_call | solution.py:295
  (2 shorter events, 0.0 us)
Async XLA Ops:
  18.3 5.4 %copy-start.5 = (f32[128,128]{1,0:T(8,128)S(1)}, f32[128,128]{1,0:T(8,128)}, u32[]{:S(2)}) copy-start(f32[128,128]{1,0:T(8,128)} %get-tuple-element.21) | copy-start | bytes 196612
  18.3 1.6 %collective-permute-start = (f32[152,128]{1,0:T(8,128)}, f32[152,128]{1,0:T(8,128)S(1)}, u32[]{:S(2)}, u32[]{:S(2)}) collective-permute-start(f32[152,128]{1,0:T(8,128)} %get-tuple-element.18), channel_id=1, source_target_pairs={{0,1},{1,0},{2,3},{3,2},{4,5},{5,4},{6,7},{7,6},{8,9},{9,8},{10,11... | collective-permute-start | bytes 233480 | tf_op jit(solution)/shard_map/ppermute | solution.py:309
  20.7 5.8 %collective-permute-start.1 = (f32[152,128]{1,0:T(8,128)S(1)}, f32[152,128]{1,0:T(8,128)S(1)}, u32[]{:S(2)}, u32[]{:S(2)}) collective-permute-start(f32[152,128]{1,0:T(8,128)S(1)} %add.9), channel_id=1, source_target_pairs={{0,2},{2,0},{1,3},{3,1},{4,6},{6,4},{5,7},{7,5},{8,10},{10,8},{9,1... | collective-permute-start | bytes 233480 | tf_op jit(solution)/shard_map/ppermute | solution.py:309
  23.7 5.1 %collective-permute-start.4 = (f32[128,128]{1,0:T(8,128)S(1)}, f32[128,128]{1,0:T(8,128)S(1)}, u32[]{:S(2)}, u32[]{:S(2)}) collective-permute-start(f32[128,128]{1,0:T(8,128)S(1)} %copy-done.5), channel_id=1, source_target_pairs={{0,2},{2,0},{1,3},{3,1},{4,6},{6,4},{5,7},{7,5},{8,10},{10,8},{9,1... | collective-permute-start | bytes 196616 | tf_op jit(solution)/shard_map/ppermute | solution.py:309
  26.6 8.5 %collective-permute-start.2 = (f32[152,128]{1,0:T(8,128)S(1)}, f32[152,128]{1,0:T(8,128)S(1)}, u32[]{:S(2)}, u32[]{:S(2)}) collective-permute-start(f32[152,128]{1,0:T(8,128)S(1)} %add.10), channel_id=1, source_target_pairs={{0,4},{4,0},{8,12},{12,8},{1,5},{5,1},{9,13},{13,9},{2,6},{6,2},{1... | collective-permute-start | bytes 233480 | tf_op jit(solution)/shard_map/ppermute | solution.py:309
  28.8 0.6 %copy-start.1 = (f32[128,128]{1,0:T(8,128)}, f32[128,128]{1,0:T(8,128)S(1)}, u32[]{:S(2)}) copy-start(f32[128,128]{1,0:T(8,128)S(1)} %collective-permute-done.4.refs_0_) | copy-start | bytes 196612
  31.1 8.6 %collective-permute-start.5 = (f32[120,256]{1,0:T(8,128)}, f32[120,256]{1,0:T(8,128)S(1)}, u32[]{:S(2)}, u32[]{:S(2)}) collective-permute-start(f32[120,256]{1,0:T(8,128)} %get-tuple-element.22), channel_id=1, source_target_pairs={{0,4},{4,8},{8,12},{1,5},{5,9},{9,13},{2,6},{6,10},{10,14},{3,7},{... | collective-permute-start | bytes 368648 | tf_op jit(solution)/shard_map/ppermute | solution.py:331
  33.8 8.2 %collective-permute-start.6 = (f32[120,256]{1,0:T(8,128)}, f32[120,256]{1,0:T(8,128)S(1)}, u32[]{:S(2)}, u32[]{:S(2)}) collective-permute-start(f32[120,256]{1,0:T(8,128)} %get-tuple-element.23), channel_id=1, source_target_pairs={{4,0},{8,4},{12,8},{5,1},{9,5},{13,9},{6,2},{10,6},{14,10},{7,3},{... | collective-permute-start | bytes 368648 | tf_op jit(solution)/shard_map/ppermute | solution.py:332
  35.1 11.1 %copy-start = (f32[152,128]{1,0:T(8,128)}, f32[152,128]{1,0:T(8,128)S(1)}, u32[]{:S(2)}) copy-start(f32[152,128]{1,0:T(8,128)S(1)} %add.11.refs_0_) | copy-start | bytes 233476
  35.1 11.1 %collective-permute-start.3 = (f32[152,128]{1,0:T(8,128)S(1)}, f32[152,128]{1,0:T(8,128)S(1)}, u32[]{:S(2)}, u32[]{:S(2)}) collective-permute-start(f32[152,128]{1,0:T(8,128)S(1)} %add.11.refs_0_), channel_id=1, source_target_pairs={{0,8},{4,12},{8,0},{12,4},{1,9},{5,13},{9,1},{13,5},{2,10},{6,14},... | collective-permute-start | bytes 233480 | tf_op jit(solution)/shard_map/ppermute | solution.py:309
  39.6 2.3 %copy-start.2 = (f32[120,256]{1,0:T(8,128)}, f32[120,256]{1,0:T(8,128)S(1)}, u32[]{:S(2)}) copy-start(f32[120,256]{1,0:T(8,128)S(1)} %collective-permute-done.5.above_ref) | copy-start | bytes 368644
  42.0 0.6 %copy-start.3 = (f32[120,256]{1,0:T(8,128)}, f32[120,256]{1,0:T(8,128)S(1)}, u32[]{:S(2)}) copy-start(f32[120,256]{1,0:T(8,128)S(1)} %collective-permute-done.6.below_ref) | copy-start | bytes 368644
  46.2 0.6 %copy-start.4 = (f32[152,128]{1,0:T(8,128)}, f32[152,128]{1,0:T(8,128)S(1)}, u32[]{:S(2)}) copy-start(f32[152,128]{1,0:T(8,128)S(1)} %collective-permute-done.3.refs_1_) | copy-start | bytes 233476

commit v2 on v1

v2 whole, which is shorter than its diff:
```python
import functools

import jax
import jax.numpy as jnp
import ml_dtypes
import numpy as np
from jax import lax
from jax.experimental import pallas as pl
from jax.experimental.pallas import tpu as pltpu
from jax.sharding import PartitionSpec as P

RADIUS = 24
BACKGROUND = 0.1
UNIT = 8
F32 = jnp.float32
BF = jnp.bfloat16
NT = (((1,), (1,)), ((), ()))


def net_kernel(sides, *refs):
    inputs, refs = refs[0:7], refs[7:]
    keep_out, send_out, src_out, tgt_out = refs[0:4]
    strip_outs, scr = refs[4:4 + sides], refs[4 + sides:]
    held, arrived, scr = scr[-8:-1], scr[-1], scr[:-8]
    copies = [pltpu.make_async_copy(a, b, arrived.at[k]) for k, (a, b) in enumerate(zip(inputs, held))]
    for copy in copies:
        copy.start()
    drv, obs, conf, mask, w1, w2, wo = held
    for copy in copies:
        copy.wait()
    rows = mask.shape[0]
    hid = w2.shape[0]
    feat = w1.shape[0]
    units = rows // UNIT
    wide = UNIT * 128
    TILE = 256
    h1s, s1s, p2s, d2s = scr[0:3], scr[3:6], scr[6:9], scr[9:12]
    xs, obf, wmf, mkf, acc_second, acc_first, acc_outg, wide_wo = scr[12:]
    w1h = (w1[...].astype(F32) * 0.5).T.astype(BF)
    w2f = w2[...].astype(F32)
    w2h = (w2f * 0.5).T.astype(BF)
    w2b = (w2f * 0.5).astype(BF)
    wo_row = wo[...].astype(F32)
    wo_col = jnp.broadcast_to(wo_row, (128, hid)).T
    wide_wo[0] = wo_col
    wide_wo[1] = 0.5 * wo_col
    sub = lax.broadcasted_iota(jnp.int32, (8, 128), 0)
    acc_second[...] = jnp.zeros_like(acc_second)
    acc_first[...] = jnp.zeros_like(acc_first)
    acc_outg[...] = jnp.zeros_like(acc_outg)

    def prepare(i, c):
        r0 = pl.multiple_of(i * 16, 16)
        x3 = jnp.swapaxes(drv[0, :, pl.ds(r0, 16), :].astype(F32), 0, 1).astype(BF)
        xs[:, pl.ds(pl.multiple_of(i * 2048, 2048), 2048)] = jnp.concatenate([x3[r] for r in range(16)], axis=1)
        return c
    lax.fori_loop(0, rows // 16, prepare, 0)
    ob = obs[0].astype(F32)
    mk = mask[...].astype(F32)
    wm = (conf[0].astype(F32) * mk).astype(BF).astype(F32)
    tg = ob * mk
    tgt_out[...] = tg
    obf[...] = ob
    wmf[...] = wm
    mkf[...] = mk

    def one(i, k, f1=True, f2=True, f3=True):
        a, b, c = k % 3, (k + 2) % 3, (k + 1) % 3
        n = wide // TILE
        if f3:
            x_old = xs[:, pl.ds(pl.multiple_of((i - 2) * wide, wide), wide)]
            d2 = d2s[c][...]
        if f1:
            x_new = xs[:, pl.ds(pl.multiple_of(jnp.minimum(i, units - 1) * wide, wide), wide)]
        def s3(j):
            sl = slice(j * TILE, (j + 1) * TILE)
            back = jnp.dot(w2b, d2[:, sl], preferred_element_type=F32)
            d1 = (back * s1s[c][:, sl]).astype(BF)
            acc_first[...] += lax.dot_general(d1, x_old[:, sl], NT, preferred_element_type=F32)
        def s1(j):
            sl = slice(j * TILE, (j + 1) * TILE)
            p1 = jnp.dot(w1h, x_new[:, sl], preferred_element_type=F32)
            t1 = jnp.tanh(p1)
            u1 = 1.0 + t1
            h1 = (p1 * u1).astype(BF)
            h1s[a][:, sl] = h1
            s1s[a][:, sl] = u1 * (1.0 + p1 * (1.0 - t1))
            p2s[a][:, sl] = jnp.dot(w2h, h1, preferred_element_type=F32)
        keep = []
        def s2(r):
            p2 = p2s[b][:, r * 128:(r + 1) * 128]
            t2 = jnp.tanh(p2)
            u2 = 1.0 + t2
            h2 = (p2 * u2).astype(BF)
            s2 = u2 * (1.0 + p2 * (1.0 - t2)) * wide_wo[1]
            keep.append((h2, s2))
        for r in range(8):
            if f2: s2(r)
            if r % (8 // n) == 0:
                if f1: s1(r // (8 // n))
                if f3: s3(r // (8 // n))
        if f3:
            acc_second[...] += lax.dot_general(h1s[c][...], d2, NT, preferred_element_type=F32)
        if not f2: return
        r0 = pl.multiple_of((i - 1) * UNIT, UNIT)
        h2w = jnp.concatenate([h for h, _ in keep], axis=1)
        scs = []
        for h2, _ in keep:
            sc = jnp.sum((h2.astype(F32) * wide_wo[0]).reshape(hid // 8, 8, 128), axis=0)
            for q in (4, 2, 1):
                sc = sc + pltpu.roll(sc, q, 0)
            scs.append(sc)
        score = scs[0]
        for r in range(1, 8):
            score = jnp.where(sub == r, scs[r], score)
        e = jnp.exp(-jnp.abs(score))
        imitated = jnp.maximum(score, 0.0) + jnp.log1p(e)
        sig = jnp.where(score >= 0, 1.0, e) / (1.0 + e)
        delta = wmf[pl.ds(r0, 8), :] * (imitated - obf[pl.ds(r0, 8), :]) * sig
        src_out[pl.ds(r0, 8), :] = mkf[pl.ds(r0, 8), :] * imitated
        mix = []
        high = delta.astype(BF).astype(F32)
        low = delta - high
        for r in range(8):
            h2, s2v = keep[r]
            d8 = jnp.broadcast_to(delta[r:r + 1], (8, 128))
            d = jnp.broadcast_to(d8[None], (hid // 8, 8, 128)).reshape(hid, 128)
            d2s[b][:, r * 128:(r + 1) * 128] = (d * s2v).astype(BF)
            mix.append(jnp.where(sub == 0, high[r:r + 1], jnp.where(sub == 1, low[r:r + 1], 0.0)))
        acc_outg[:, 0:8] += lax.dot_general(
            h2w, jnp.concatenate(mix, axis=1).astype(BF), NT, preferred_element_type=F32
        )

    one(0, 0, True, False, False)
    one(1, 1, True, True, False)
    def body(t, c):
        for k in range(3):
            one(t * 3 + 2 + k, 2 + k)
        return c
    loops = (units - 1 + 2) // 3
    lax.fori_loop(0, loops, body, 0)
    assert loops * 3 + 1 == units
    one(units + 1, units + 1, False, False, True)

    src = src_out[...]
    og = jnp.sum(acc_outg[...].T, axis=0, keepdims=True)
    me = lax.axis_index("maps")
    tot = lambda v: jnp.sum(jnp.sum(v, axis=1, keepdims=True), axis=0, keepdims=True)
    extra = jnp.where(sub == 0, og, 0.0)
    extra = jnp.where(sub == 1, tot(wmf[...]), extra)
    extra = jnp.where(sub == 2 + me, tot(src), extra)
    extra = jnp.where(sub == 4 + me, tot(tgt_out[...]), extra)
    second = acc_second[...]
    cut = hid // 2
    upper = jnp.concatenate([second[0:cut], extra, jnp.zeros((feat - 8, 128), F32)], axis=0)
    lower = jnp.concatenate([second[cut:hid], acc_first[...].T], axis=0)
    keep_out[...] = jnp.where(me == 0, upper, lower)
    send_out[...] = jnp.where(me == 0, lower, upper)
    if sides:
        lanes = lax.broadcasted_iota(jnp.int32, (rows, 128), 1)
        left, right = edge_strips(src, tgt_out[...], lanes)
        strips = [right, left]
        if sides == 1:
            strips = [jnp.where(lax.axis_index("cols") == 0, right, left)]
        for ref, strip in zip(strip_outs, strips):
            ref[...] = strip.astype(BF)


def vmem(*shape, dtype=F32):
    return pltpu.VMEM(shape, dtype)


def here(*values):
    return [pltpu.with_memory_space_constraint(value, pltpu.VMEM) for value in values]


PARAMS = pltpu.CompilerParams(vmem_limit_bytes=24 << 20)


def net(drivers, observed, confidence, land_mask, w1, w2, wo, sides):
    feat, hid = w1.shape
    rows, cols = land_mask.shape
    wide = UNIT * cols
    given = (drivers, observed, confidence, land_mask, w1, w2, wo.reshape(1, hid))
    return pl.pallas_call(
        functools.partial(net_kernel, sides),
        out_shape=[vmem(hid // 2 + feat, 128)] * 2
        + [vmem(rows, cols)] * 2
        + [vmem(rows, cols, dtype=BF)] * sides,
        scratch_shapes=[vmem(hid, wide, dtype=BF)] * 3
        + [vmem(hid, wide)] * 6
        + [vmem(hid, wide, dtype=BF)] * 3
        + [vmem(feat, rows * cols, dtype=BF)]
        + [vmem(rows, cols)] * 3
        + [vmem(hid, hid), vmem(hid, feat), vmem(hid, 128), vmem(2, hid, 128)]
        + [vmem(*value.shape, dtype=value.dtype) for value in given]
        + [pltpu.SemaphoreType.DMA((len(given),))],
        in_specs=[pl.BlockSpec(memory_space=pl.ANY)] * len(given),
        compiler_params=PARAMS,
        name="net",
    )(*[pltpu.with_memory_space_constraint(value, pltpu.HBM) for value in given])


def edge_strips(src, tgt, lane):
    right = jnp.where(lane >= 128 - 3 * RADIUS, src, pltpu.roll(tgt, 2 * RADIUS, 1))
    left = jnp.where(lane < 3 * RADIUS, src, pltpu.roll(tgt, 128 - 2 * RADIUS, 1))
    return left, right


def widen(src, tgt, strips):
    if not strips:
        return src, tgt
    lane = lax.broadcasted_iota(jnp.int32, src.shape, 1)
    first, last = strips[0][...].astype(F32), strips[-1][...].astype(F32)
    ls = jnp.where(lane >= 128 - 3 * RADIUS, first, 0.0)
    lt = jnp.where(lane >= 128 - 2 * RADIUS, pltpu.roll(first, 128 - 2 * RADIUS, 1), 0.0)
    rs = jnp.where(lane < 3 * RADIUS, last, 0.0)
    rt = jnp.where(lane < 2 * RADIUS, pltpu.roll(last, 2 * RADIUS, 1), 0.0)
    if len(strips) == 2:
        return jnp.concatenate([ls, src, rs], axis=1), jnp.concatenate([lt, tgt, rt], axis=1)
    at_left = lax.axis_index("cols") == 0
    return (
        jnp.concatenate([jnp.where(at_left, src, ls), jnp.where(at_left, rs, src)], axis=1),
        jnp.concatenate([jnp.where(at_left, tgt, lt), jnp.where(at_left, rt, tgt)], axis=1),
    )


def halo_kernel(src_ref, tgt_ref, *refs):
    strips, (up_ref, down_ref) = refs[:-2], refs[-2:]
    src, tgt = widen(src_ref[...], tgt_ref[...], strips)
    rows = src.shape[0]
    far, near = rows - 2 * RADIUS, 2 * RADIUS
    up_ref[...] = jnp.concatenate([src[0:far], tgt[0:near]], axis=0).astype(BF)
    down_ref[...] = jnp.concatenate([src[rows - far:], tgt[rows - near:]], axis=0).astype(BF)


def halo(src, tgt, strips):
    rows, cols = src.shape
    return pl.pallas_call(
        halo_kernel,
        out_shape=[vmem(rows, cols * (1 + len(strips)), dtype=BF)] * 2,
        compiler_params=PARAMS,
        name="halo",
    )(*here(src, tgt, *strips))


def parts(value):
    high = value.astype(BF)
    return high, (value - high.astype(F32)).astype(BF)


def product(left, right):
    (lh, ll), (rh, rl) = left, right
    dot = functools.partial(jnp.dot, preferred_element_type=F32)
    return dot(lh, rh) + (dot(lh, rl) + dot(ll, rh))


def sinkhorn_kernel(src_ref, tgt_ref, above_ref, below_ref, brow_ref, bcol_ref, krow_ref, kcol_ref, *refs):
    strips = refs[:-2]
    source_out, target_out = refs[-2:]
    sides = len(strips)
    far, near = 3 * RADIUS, 2 * RADIUS
    rows, wide = above_ref.shape
    rows_at, cols_at = lax.axis_index("rows"), lax.axis_index("cols")
    row_end, col_end = lax.axis_size("rows") - 1, lax.axis_size("cols") - 1
    src, tgt = widen(src_ref[...], tgt_ref[...], strips)
    above, below = above_ref[...].astype(F32), below_ref[...].astype(F32)
    source = jnp.concatenate([above[rows - near - far:rows - near], src, below[0:far]], axis=0)
    target = jnp.concatenate([above[rows - near:], tgt, below[rows - near:]], axis=0)
    own = (0, cols_at * 128, 128)[sides]

    def background(field, reach):
        row = lax.broadcasted_iota(jnp.int32, field.shape, 0)
        lane = lax.broadcasted_iota(jnp.int32, field.shape, 1)
        inside = (row >= jnp.where(rows_at == 0, reach, 0)) & (
            row < jnp.where(rows_at == row_end, reach + rows, 2 * reach + rows)
        )
        if sides:
            inside &= (lane >= own - jnp.where(cols_at == 0, 0, reach)) & (
                lane < own + 128 + jnp.where(cols_at == col_end, 0, reach)
            )
        return jnp.where(inside, field + BACKGROUND, 0.0)

    source, target = background(source, far), background(target, near)
    krow = 1.0 - (rows_at == 0).astype(F32) * krow_ref[0] - (rows_at == row_end).astype(F32) * krow_ref[1]
    if sides == 2:
        col_first, col_last = (cols_at == 0).astype(F32), (cols_at == col_end).astype(F32)
        kcol = 1.0 - col_first * kcol_ref[0:1, :] - col_last * kcol_ref[1:2, :]
    else:
        kcol = 1.0 - kcol_ref[0:1, :] - kcol_ref[1:2, :]
    krow = jnp.concatenate([krow] * (1 + sides), axis=1)
    brow = (brow_ref[0], brow_ref[1])
    bcol = (bcol_ref[0], bcol_ref[1])
    if sides == 1:
        last_bcol = tuple(jnp.where(cols_at == 0, band[:, 0:128], band[:, 128:256]) for band in bcol)
    else:
        last_bcol = tuple(band[:, own:own + 128] for band in bcol)

    def smooth(field, count, columns):
        bands = tuple(band[0:count, 0:count + near] for band in brow)
        return product(parts(product(bands, parts(field))), columns)

    def ratio(top, bottom):
        inside = top > 0.0
        return jnp.where(inside, top / jnp.where(inside, bottom, 1.0), 0.0)

    scaling = source / (krow * kcol)
    scaling = ratio(target, smooth(scaling, rows + 2 * near, bcol))
    scaling = ratio(source[near:near + rows + near], smooth(scaling, rows + near, bcol))
    bottom = smooth(scaling, rows, last_bcol)
    middle = scaling[RADIUS:RADIUS + rows]
    if sides == 1:
        source_out[...] = jnp.where(cols_at == 0, middle[:, 0:128], middle[:, 128:256])
    else:
        source_out[...] = middle[:, own:own + 128]
    target_out[...] = (tgt_ref[...] + BACKGROUND) / bottom


def split_table(table):
    high = table.astype(ml_dtypes.bfloat16)
    low = (table - high.astype(np.float64)).astype(ml_dtypes.bfloat16)
    return np.stack([high, low])


def taps():
    offsets = np.arange(-RADIUS, RADIUS + 1, dtype=np.float64)
    weights = np.exp(-4.5 * offsets * offsets / (RADIUS * RADIUS))
    return weights / weights.sum()


def tails(start, count, end):
    weights = taps()
    before, after = np.zeros(count), np.zeros(count)
    for at in range(count):
        if at >= start:
            before[at] = weights[: max(0, RADIUS - (at - start))].sum()
        if at < end:
            after[at] = weights[: max(0, RADIUS - (end - 1 - at))].sum()
    return np.stack([before, after])


def sinkhorn(src, tgt, above, below, strips):
    rows, cols = src.shape
    sides = len(strips)
    wide = cols * (1 + sides)
    weights = taps()

    def toeplitz(count_out, count_in, shift):
        offset = np.arange(count_in)[None, :] - np.arange(count_out)[:, None] + shift
        inside = (offset >= 0) & (offset <= 2 * RADIUS)
        return np.where(inside, weights[np.clip(offset, 0, 2 * RADIUS)], 0.0)

    brow = split_table(toeplitz(rows + 4 * RADIUS, rows + 6 * RADIUS, 0))
    bcol = split_table(toeplitz(wide, wide, RADIUS))
    krow = tails(3 * RADIUS, rows + 6 * RADIUS, 3 * RADIUS + rows)
    krow = np.broadcast_to(krow[:, :, None], krow.shape + (128,)).astype(np.float32)
    kcol = tails(cols, wide, 2 * cols) if sides == 2 else tails(0, wide, wide)
    kcol = np.concatenate([kcol, np.zeros((6, wide))]).astype(np.float32)
    tables = [jnp.asarray(table) for table in (brow, bcol, krow, kcol)]
    return pl.pallas_call(
        sinkhorn_kernel,
        out_shape=[vmem(rows, cols)] * 2,
        compiler_params=PARAMS,
        cost_estimate=pl.CostEstimate(flops=2000000000, bytes_accessed=1000000, transcendentals=0),
        name="sinkhorn",
    )(*here(src, tgt, above, below), *here(*tables), *here(*strips))


def finish_kernel(cells, hid, feat, mine_ref, other_ref, source_ref, target_ref, *outs):
    first_out, second_out, output_out, source_out, target_out = outs
    me = lax.axis_index("maps")
    mine, other = mine_ref[...], other_ref[...]
    upper, lower = jnp.where(me == 0, mine, other), jnp.where(me == 0, other, mine)
    cut = hid // 2
    tail = upper[cut:cut + 8]
    inverse = 1.0 / tail[1:2]
    second_out[0:cut, :] = upper[0:cut] * inverse
    second_out[cut:hid, :] = lower[0:cut] * inverse
    first_out[...] = lower[cut:cut + feat] * inverse
    output_out[...] = tail[0:1] * inverse
    source_mean = jnp.where(me == 0, tail[2:3], tail[3:4]) * (1.0 / cells) + BACKGROUND
    target_mean = jnp.where(me == 0, tail[4:5], tail[5:6]) * (1.0 / cells) + BACKGROUND
    ratio = source_mean / target_mean
    source_out[0] = source_ref[...] * (1.0 / (source_mean * ratio))
    target_out[0] = target_ref[...] * (ratio * ratio)


def finish(mine, other, source, target, cells, hid, feat):
    shape = jax.ShapeDtypeStruct((1,) + source.shape, F32)
    return pl.pallas_call(
        functools.partial(finish_kernel, cells, hid, feat),
        out_shape=(
            jax.ShapeDtypeStruct((feat, hid), F32),
            jax.ShapeDtypeStruct((hid, hid), F32),
            jax.ShapeDtypeStruct((1, hid), F32),
            shape,
            shape,
        ),
        compiler_params=PARAMS,
        name="finish",
    )(*here(mine, other, source, target))


def swap(value, axis, step):
    return lax.ppermute(value, axis, [(i, i ^ step) for i in range(lax.axis_size(axis))])


def shift(value, axis, step):
    count = lax.axis_size(axis)
    pairs = [(i, i + step) for i in range(count) if 0 <= i + step < count]
    return lax.ppermute(value, axis, pairs)


def powers(axis):
    return [1 << k for k in range((lax.axis_size(axis) - 1).bit_length())]


def local(
    drivers, observed, confidence, land_mask, ownership, first_layer, second_layer, output_layer
):
    feat, hid = first_layer.shape
    row_count, col_count = lax.axis_size("rows"), lax.axis_size("cols")
    cells = land_mask.size * row_count * col_count
    sides = min(col_count - 1, 2)
    keep, send, src, tgt, *strips = net(
        drivers, observed, confidence, land_mask, first_layer, second_layer, output_layer, sides
    )
    total = keep + swap(send, "maps", 1)
    if sides == 1:
        strips = [swap(strips[0], "cols", 1)]
    elif sides == 2:
        strips = [shift(strips[0], "cols", 1), shift(strips[1], "cols", -1)]
    for step in powers("cols"):
        total = total + swap(total, "cols", step)
    total, src, tgt, *strips = lax.optimization_barrier((total, src, tgt, *strips))
    up, down = halo(src, tgt, strips)
    above, below = shift(down, "rows", 1), shift(up, "rows", -1)
    for at, step in enumerate(powers("rows")):
        total = total + swap(total, "rows", step)
        if at == 0:
            total, above, below = lax.optimization_barrier((total, above, below))
    source, target = sinkhorn(src, tgt, above, below, strips)
    other = swap(total, "maps", 1)
    first, second, output, source, target = finish(total, other, source, target, cells, hid, feat)
    return first, second, output.reshape(hid), source, target


def solution(mesh):
    in_specs = (
        P(("groups", "maps"), None, "rows", "cols"),
        P(("groups", "maps"), "rows", "cols"),
        P(("groups", "maps"), "rows", "cols"),
        P(("groups", "rows"), "cols"),
        P(("groups", "rows"), "cols"),
        P(),
        P(),
        P(),
    )
    out_specs = (
        P("groups", None),
        P("groups", None),
        P("groups"),
        P(("groups", "maps"), "rows", "cols"),
        P(("groups", "maps"), "rows", "cols"),
    )
    return jax.shard_map(local, mesh=mesh, in_specs=in_specs, out_specs=out_specs, check_vma=False)
```

time: 48.9 us -> 41 us (0.84)
  Pallas kernels: 24.6 us -> 16.7 us
  waiting for transfers between devices: 6.26 us -> 9.28 us
  local copies, waits for them, and re-layouts: 1.91 us -> 0.02 us
  other arithmetic: 0.92 us -> 0.03 us
    pallas_call x3, Pallas kernels: 23 us -> 16 us  [the longest x1 14.1 us: net(): pl.pallas_call(functools.partial(net_kernel, sides), out_shape=[vmem(hid...]
    ppermute x5 -> x6, waiting for transfers between devices: 3.94 us -> 9.27 us  [swap(): lax.ppermute(value, axis, [(i, i ^ step) for i in range(lax.axis_size(axi...]
    ppermute x2, waiting for transfers between devices: 2.32 us -> 0.01 us  [shift(): return lax.ppermute(value, axis, pairs)]
    unnamed x12 -> x8, local copies, waits for them, and re-layouts: 1.91 us -> 0.02 us
    pallas_call x1, Pallas kernels: 1.64 us -> 0.71 us  [finish(): pl.pallas_call(functools.partial(finish_kernel, cells, hid, feat), out_sh...]
    add x3 -> x4, other arithmetic: 0.92 us -> 0.03 us  [the longest x2 0.01 us: local(): total = total + swap(total, 'rows', step)]
    ppermute x5 -> x6, starting transfers between devices: 10.2 us -> 9.3 us  [swap(): lax.ppermute(value, axis, [(i, i ^ step) for i in range(lax.axis_size(axi...]
    ppermute x2, starting transfers between devices: 3.98 us -> 4.78 us  [shift(): return lax.ppermute(value, axis, pairs)]
  transfers between devices with their start and end apart: 7 -> 8, of which waited for: 3 -> 5; matrix products, arithmetic and copies ran while one was open for 0% -> 0% of each run, Pallas kernels for 11% -> 4%
where the time goes in v2:
time: 41 us; the launch traced here: 40.8 us
  Pallas kernels  16.7 us (41%)
  starting transfers between devices  14.1 us (34%)
  waiting for transfers between devices  9.28 us (23%)
  between operations  0.76 us (2%)
    pallas_call x1, Pallas kernels, net(): pl.pallas_call(functools.partial(net_kernel, sides), out_shape=[vmem(hid...  14.1 us
    ppermute x6, starting transfers between devices, swap(): lax.ppermute(value, axis, [(i, i ^ step) for i in range(lax.axis_size(axi...  9.3 us
    ppermute x6, waiting for transfers between devices, swap(): lax.ppermute(value, axis, [(i, i ^ step) for i in range(lax.axis_size(axi...  9.27 us
    ppermute x2, starting transfers between devices, shift(): return lax.ppermute(value, axis, pairs)  4.78 us
    pallas_call x1, Pallas kernels, sinkhorn(): pl.pallas_call(sinkhorn_kernel, out_shape=[vmem(rows, cols)] * 2, compile...  1.74 us
  transfers between devices with their start and end apart: 8, of which 5 were waited for; matrix products, arithmetic and copies ran while one was open for 0% of the time, Pallas kernels for 4%

profile of v2, /device:TPU:0, one launch (start us, length us, event | category | flops | bytes accessed | tf_op | source)
XLA Modules:
  0.0 40.8 jit_solution(2456850420689086737)
XLA Ops:
  0.6 0.0 copy-start.2
  0.6 14.1 %net.1 = (f32[80,128]{1,0:T(8,128)S(1)}, f32[80,128]{1,0:T(8,128)S(1)}, f32[128,128]{1,0:T(8,128)S(1)}, f32[128,128]{1,0:T(8,128)S(1)}, bf16[128,128]{1,0:T(8,128)(2,1)S(1)}) custom-call(bf16[1,16,128,128]{3,2,1,0:T(8,128)(2,1)} %refs_0_.1, bf16[1,128,128]{2,1,0:T(8,128)(2,1)} %refs_1_.1, bf16[1,128,128]{2,1,0:T(8,128)(2,1)} %refs_2_.1, s32[128,128]{1,0:T(8,128)} %refs_3_.1, ...), custom_call_target="tpu_custom_call" | custom-call | tf_op jit(solution)/shard_map/net/pallas_call | solution.py:185
  14.8 0.0 copy-start
  14.8 0.5 %collective-permute-start = (f32[80,128]{1,0:T(8,128)S(1)}, f32[80,128]{1,0:T(8,128)S(1)}, u32[]{:S(2)}, u32[]{:S(2)}) collective-permute-start(f32[80,128]{1,0:T(8,128)S(1)} %get-tuple-element.27), channel_id=1, source_target_pairs={{0,1},{1,0},{2,3},{3,2},{4,5},{5,4},{6,7},{7,6},{8,9},{9,8},{10,11... | collective-permute-start | bytes 122888 | tf_op jit(solution)/shard_map/ppermute | solution.py:405
  15.3 0.9 %collective-permute-done = f32[80,128]{1,0:T(8,128)S(1)} collective-permute-done((f32[80,128]{1,0:T(8,128)S(1)}, f32[80,128]{1,0:T(8,128)S(1)}, u32[]{:S(2)}, u32[]{:S(2)}) %collective-permute-start) | collective-permute-done | bytes 40992 | tf_op jit(solution)/shard_map/ppermute | solution.py:405
  16.2 0.0 copy-start.1
  16.2 2.9 %collective-permute-start.1 = (f32[80,128]{1,0:T(8,128)S(1)}, f32[80,128]{1,0:T(8,128)S(1)}, u32[]{:S(2)}, u32[]{:S(2)}) collective-permute-start(f32[80,128]{1,0:T(8,128)S(1)} %add.12), channel_id=1, source_target_pairs={{0,2},{2,0},{1,3},{3,1},{4,6},{6,4},{5,7},{7,5},{8,10},{10,8},{9,1... | collective-permute-start | bytes 122888 | tf_op jit(solution)/shard_map/ppermute | solution.py:405
  19.1 0.1 collective-permute-start.2
  19.2 1.9 %collective-permute-done.1 = f32[80,128]{1,0:T(8,128)S(1)} collective-permute-done((f32[80,128]{1,0:T(8,128)S(1)}, f32[80,128]{1,0:T(8,128)S(1)}, u32[]{:S(2)}, u32[]{:S(2)}) %collective-permute-start.1) | collective-permute-done | bytes 40992 | tf_op jit(solution)/shard_map/ppermute | solution.py:405
  21.1 1.9 %collective-permute-done.2.refs_0_ = bf16[128,128]{1,0:T(8,128)(2,1)S(1)} collective-permute-done((bf16[128,128]{1,0:T(8,128)(2,1)S(1)}, bf16[128,128]{1,0:T(8,128)(2,1)S(1)}, u32[]{:S(2)}, u32[]{:S(2)}) %collective-permute-start.2) | collective-permute-done | bytes 32800 | tf_op jit(solution)/shard_map/ppermute | solution.py:405
  23.0 0.1 halo.1
  23.1 3.5 %collective-permute-start.4 = (bf16[128,256]{1,0:T(8,128)(2,1)S(1)}, bf16[128,256]{1,0:T(8,128)(2,1)S(1)}, u32[]{:S(2)}, u32[]{:S(2)}) collective-permute-start(bf16[128,256]{1,0:T(8,128)(2,1)S(1)} %get-tuple-element.35), channel_id=1, source_target_pairs={{0,4},{4,8},{8,12},{1,5},{5,9},{9,13},{2,6},{6,10},{10,14},{3,7},{... | collective-permute-start | bytes 196616 | tf_op jit(solution)/shard_map/ppermute | solution.py:411
  26.6 1.3 %collective-permute-start.5 = (bf16[128,256]{1,0:T(8,128)(2,1)S(1)}, bf16[128,256]{1,0:T(8,128)(2,1)S(1)}, u32[]{:S(2)}, u32[]{:S(2)}) collective-permute-start(bf16[128,256]{1,0:T(8,128)(2,1)S(1)} %get-tuple-element.36), channel_id=1, source_target_pairs={{4,0},{8,4},{12,8},{5,1},{9,5},{13,9},{6,2},{10,6},{14,10},{7,3},{... | collective-permute-start | bytes 196616 | tf_op jit(solution)/shard_map/ppermute | solution.py:411
  27.9 2.7 %collective-permute-start.3 = (f32[80,128]{1,0:T(8,128)S(1)}, f32[80,128]{1,0:T(8,128)S(1)}, u32[]{:S(2)}, u32[]{:S(2)}) collective-permute-start(f32[80,128]{1,0:T(8,128)S(1)} %add.13), channel_id=1, source_target_pairs={{0,4},{4,0},{8,12},{12,8},{1,5},{5,1},{9,13},{13,9},{2,6},{6,2},{1... | collective-permute-start | bytes 122888 | tf_op jit(solution)/shard_map/ppermute | solution.py:405
  30.6 2.6 %collective-permute-done.3 = f32[80,128]{1,0:T(8,128)S(1)} collective-permute-done((f32[80,128]{1,0:T(8,128)S(1)}, f32[80,128]{1,0:T(8,128)S(1)}, u32[]{:S(2)}, u32[]{:S(2)}) %collective-permute-start.3) | collective-permute-done | bytes 40992 | tf_op jit(solution)/shard_map/ppermute | solution.py:405
  33.2 0.0 copy-start.3
  33.2 0.0 collective-permute-done.4.above_ref
  33.2 0.0 collective-permute-done.5.below_ref
  33.2 3.1 %collective-permute-start.6 = (f32[80,128]{1,0:T(8,128)S(1)}, f32[80,128]{1,0:T(8,128)S(1)}, u32[]{:S(2)}, u32[]{:S(2)}) collective-permute-start(f32[80,128]{1,0:T(8,128)S(1)} %add.14), channel_id=1, source_target_pairs={{0,8},{4,12},{8,0},{12,4},{1,9},{5,13},{9,1},{13,5},{2,10},{6,14},... | collective-permute-start | bytes 122888 | tf_op jit(solution)/shard_map/ppermute | solution.py:405
  36.3 2.0 %collective-permute-done.6 = f32[80,128]{1,0:T(8,128)S(1)} collective-permute-done((f32[80,128]{1,0:T(8,128)S(1)}, f32[80,128]{1,0:T(8,128)S(1)}, u32[]{:S(2)}, u32[]{:S(2)}) %collective-permute-start.6) | collective-permute-done | bytes 40992 | tf_op jit(solution)/shard_map/ppermute | solution.py:405
  38.3 0.0 collective-permute-start.7
  38.3 0.0 copy-done.2
  38.3 0.0 copy-done
  38.3 0.0 copy-done.1
  38.4 0.0 copy-done.3
  38.4 1.7 %sinkhorn.1 = (f32[128,128]{1,0:T(8,128)S(1)}, f32[128,128]{1,0:T(8,128)S(1)}) custom-call(f32[128,128]{1,0:T(8,128)S(1)} %get-tuple-element.32.src_ref, f32[128,128]{1,0:T(8,128)S(1)} %get-tuple-element.33.tgt_ref, bf16[128,256]{1,0:T(8,128)(2,1)S(1)} %collective-permute-done.4.above_ref, bf16[128,256]{1,0:T(8,128)(2,1)S(1)} %collective-permute-done.5.below_ref, ...), custom_call_target="tpu_custom_call" | custom-call | flops 2000000000 | bytes 1000000 | tf_op jit(solution)/shard_map/sinkhorn/pallas_call | solution.py:360
  40.1 0.0 collective-permute-done.7.other_ref
  40.1 0.7 %finish.1 = (f32[16,128]{1,0:T(8,128)}, f32[128,128]{1,0:T(8,128)}, f32[1,128]{1,0:T(1,128)}, f32[1,128,128]{2,1,0:T(8,128)}, f32[1,128,128]{2,1,0:T(8,128)}) custom-call(f32[80,128]{1,0:T(8,128)S(1)} %add.15.mine_ref, f32[80,128]{1,0:T(8,128)S(1)} %collective-permute-done.7.other_ref, f32[128,128]{1,0:T(8,128)S(1)} %get-tuple-element.40.source_ref, ...), custom_call_target="tpu_custom_call" | custom-call | tf_op jit(solution)/shard_map/finish/pallas_call | solution.py:390
  (4 shorter events, 0.0 us)
Async XLA Ops:
  0.6 37.7 %copy-start.2 = (bf16[2,256,256]{2,1,0:T(8,128)(2,1)S(1)}, bf16[2,256,256]{2,1,0:T(8,128)(2,1)}, u32[]{:S(2)}) copy-start(bf16[2,256,256]{2,1,0:T(8,128)(2,1)} %constant.9.clone.bcol_ref) | copy-start | bytes 786436
  14.8 23.6 %copy-start = (bf16[2,224,272]{2,1,0:T(8,128)(2,1)S(1)}, bf16[2,224,272]{2,1,0:T(8,128)(2,1)}, u32[]{:S(2)}) copy-start(bf16[2,224,272]{2,1,0:T(8,128)(2,1)} %constant.8.clone.brow_ref) | copy-start | bytes 731140
  14.8 1.4 %collective-permute-start = (f32[80,128]{1,0:T(8,128)S(1)}, f32[80,128]{1,0:T(8,128)S(1)}, u32[]{:S(2)}, u32[]{:S(2)}) collective-permute-start(f32[80,128]{1,0:T(8,128)S(1)} %get-tuple-element.27), channel_id=1, source_target_pairs={{0,1},{1,0},{2,3},{3,2},{4,5},{5,4},{6,7},{7,6},{8,9},{9,8},{10,11... | collective-permute-start | bytes 122888 | tf_op jit(solution)/shard_map/ppermute | solution.py:405
  16.2 22.2 %copy-start.1 = (f32[2,272,128]{2,1,0:T(8,128)S(1)}, f32[2,272,128]{2,1,0:T(8,128)}, u32[]{:S(2)}) copy-start(f32[2,272,128]{2,1,0:T(8,128)} %constant.10.clone.krow_ref) | copy-start | bytes 835588
  16.2 4.9 %collective-permute-start.1 = (f32[80,128]{1,0:T(8,128)S(1)}, f32[80,128]{1,0:T(8,128)S(1)}, u32[]{:S(2)}, u32[]{:S(2)}) collective-permute-start(f32[80,128]{1,0:T(8,128)S(1)} %add.12), channel_id=1, source_target_pairs={{0,2},{2,0},{1,3},{3,1},{4,6},{6,4},{5,7},{7,5},{8,10},{10,8},{9,1... | collective-permute-start | bytes 122888 | tf_op jit(solution)/shard_map/ppermute | solution.py:405
  19.1 3.9 %collective-permute-start.2 = (bf16[128,128]{1,0:T(8,128)(2,1)S(1)}, bf16[128,128]{1,0:T(8,128)(2,1)S(1)}, u32[]{:S(2)}, u32[]{:S(2)}) collective-permute-start(bf16[128,128]{1,0:T(8,128)(2,1)S(1)} %get-tuple-element.30), channel_id=1, source_target_pairs={{0,2},{2,0},{1,3},{3,1},{4,6},{6,4},{5,7},{7,5},{8,10},{10,8},{9,1... | collective-permute-start | bytes 98312 | tf_op jit(solution)/shard_map/ppermute | solution.py:405
  23.1 10.1 %collective-permute-start.4 = (bf16[128,256]{1,0:T(8,128)(2,1)S(1)}, bf16[128,256]{1,0:T(8,128)(2,1)S(1)}, u32[]{:S(2)}, u32[]{:S(2)}) collective-permute-start(bf16[128,256]{1,0:T(8,128)(2,1)S(1)} %get-tuple-element.35), channel_id=1, source_target_pairs={{0,4},{4,8},{8,12},{1,5},{5,9},{9,13},{2,6},{6,10},{10,14},{3,7},{... | collective-permute-start | bytes 196616 | tf_op jit(solution)/shard_map/ppermute | solution.py:411
  26.6 6.6 %collective-permute-start.5 = (bf16[128,256]{1,0:T(8,128)(2,1)S(1)}, bf16[128,256]{1,0:T(8,128)(2,1)S(1)}, u32[]{:S(2)}, u32[]{:S(2)}) collective-permute-start(bf16[128,256]{1,0:T(8,128)(2,1)S(1)} %get-tuple-element.36), channel_id=1, source_target_pairs={{4,0},{8,4},{12,8},{5,1},{9,5},{13,9},{6,2},{10,6},{14,10},{7,3},{... | collective-permute-start | bytes 196616 | tf_op jit(solution)/shard_map/ppermute | solution.py:411
  27.9 5.3 %collective-permute-start.3 = (f32[80,128]{1,0:T(8,128)S(1)}, f32[80,128]{1,0:T(8,128)S(1)}, u32[]{:S(2)}, u32[]{:S(2)}) collective-permute-start(f32[80,128]{1,0:T(8,128)S(1)} %add.13), channel_id=1, source_target_pairs={{0,4},{4,0},{8,12},{12,8},{1,5},{5,1},{9,13},{13,9},{2,6},{6,2},{1... | collective-permute-start | bytes 122888 | tf_op jit(solution)/shard_map/ppermute | solution.py:405
  33.2 5.2 %copy-start.3 = (f32[8,256]{1,0:T(8,128)S(1)}, f32[8,256]{1,0:T(8,128)}, u32[]{:S(2)}) copy-start(f32[8,256]{1,0:T(8,128)} %constant.11.clone.kcol_ref) | copy-start | bytes 24580
  33.2 5.1 %collective-permute-start.6 = (f32[80,128]{1,0:T(8,128)S(1)}, f32[80,128]{1,0:T(8,128)S(1)}, u32[]{:S(2)}, u32[]{:S(2)}) collective-permute-start(f32[80,128]{1,0:T(8,128)S(1)} %add.14), channel_id=1, source_target_pairs={{0,8},{4,12},{8,0},{12,4},{1,9},{5,13},{9,1},{13,5},{2,10},{6,14},... | collective-permute-start | bytes 122888 | tf_op jit(solution)/shard_map/ppermute | solution.py:405
  38.3 1.8 %collective-permute-start.7 = (f32[80,128]{1,0:T(8,128)S(1)}, f32[80,128]{1,0:T(8,128)S(1)}, u32[]{:S(2)}, u32[]{:S(2)}) collective-permute-start(f32[80,128]{1,0:T(8,128)S(1)} %add.15.mine_ref), channel_id=1, source_target_pairs={{0,1},{1,0},{2,3},{3,2},{4,5},{5,4},{6,7},{7,6},{8,9},{9,8},{10,11... | collective-permute-start | bytes 122888 | tf_op jit(solution)/shard_map/ppermute | solution.py:405

commit v3 on v2

--- a/solution.py
+++ b/solution.py
@@ -226,12 +226,15 @@
 
 
 def halo_kernel(src_ref, tgt_ref, *refs):
-    strips, (up_ref, down_ref) = refs[:-2], refs[-2:]
+    strips, (near_ref, far_ref) = refs[:-2], refs[-2:]
     src, tgt = widen(src_ref[...], tgt_ref[...], strips)
     rows = src.shape[0]
     far, near = rows - 2 * RADIUS, 2 * RADIUS
-    up_ref[...] = jnp.concatenate([src[0:far], tgt[0:near]], axis=0).astype(BF)
-    down_ref[...] = jnp.concatenate([src[rows - far:], tgt[rows - near:]], axis=0).astype(BF)
+    up = jnp.concatenate([src[0:far], tgt[0:near]], axis=0)
+    down = jnp.concatenate([src[rows - far:], tgt[rows - near:]], axis=0)
+    even = lax.axis_index("rows") % 2 == 0
+    near_ref[...] = jnp.where(even, down, up).astype(BF)
+    far_ref[...] = jnp.where(even, up, down).astype(BF)
 
 
 def halo(src, tgt, strips):
@@ -255,16 +258,18 @@
     return dot(lh, rh) + (dot(lh, rl) + dot(ll, rh))
 
 
-def sinkhorn_kernel(src_ref, tgt_ref, above_ref, below_ref, brow_ref, bcol_ref, krow_ref, kcol_ref, *refs):
+def sinkhorn_kernel(src_ref, tgt_ref, pair_ref, next_ref, brow_ref, bcol_ref, krow_ref, kcol_ref, *refs):
     strips = refs[:-2]
     source_out, target_out = refs[-2:]
     sides = len(strips)
     far, near = 3 * RADIUS, 2 * RADIUS
-    rows, wide = above_ref.shape
+    rows, wide = pair_ref.shape
     rows_at, cols_at = lax.axis_index("rows"), lax.axis_index("cols")
     row_end, col_end = lax.axis_size("rows") - 1, lax.axis_size("cols") - 1
     src, tgt = widen(src_ref[...], tgt_ref[...], strips)
-    above, below = above_ref[...].astype(F32), below_ref[...].astype(F32)
+    pair, following = pair_ref[...].astype(F32), next_ref[...].astype(F32)
+    even = rows_at % 2 == 0
+    above, below = jnp.where(even, following, pair), jnp.where(even, pair, following)
     source = jnp.concatenate([above[rows - near - far:rows - near], src, below[0:far]], axis=0)
     target = jnp.concatenate([above[rows - near:], tgt, below[rows - near:]], axis=0)
     own = (0, cols_at * 128, 128)[sides]
@@ -339,7 +344,7 @@
     return np.stack([before, after])
 
 
-def sinkhorn(src, tgt, above, below, strips):
+def sinkhorn(src, tgt, pair, following, strips):
     rows, cols = src.shape
     sides = len(strips)
     wide = cols * (1 + sides)
@@ -363,7 +368,7 @@
         compiler_params=PARAMS,
         cost_estimate=pl.CostEstimate(flops=2000000000, bytes_accessed=1000000, transcendentals=0),
         name="sinkhorn",
-    )(*here(src, tgt, above, below), *here(*tables), *here(*strips))
+    )(*here(src, tgt, pair, following), *here(*tables), *here(*strips))
 
 
 def finish_kernel(cells, hid, feat, mine_ref, other_ref, source_ref, target_ref, *outs):
@@ -408,6 +413,12 @@
 def shift(value, axis, step):
     count = lax.axis_size(axis)
     pairs = [(i, i + step) for i in range(count) if 0 <= i + step < count]
+    return lax.ppermute(value, axis, pairs)
+
+
+def exchange(value, axis, start):
+    count = lax.axis_size(axis)
+    pairs = [pair for i in range(start, count - 1, 2) for pair in ((i, i + 1), (i + 1, i))]
     return lax.ppermute(value, axis, pairs)
 
 
@@ -433,13 +444,14 @@
     for step in powers("cols"):
         total = total + swap(total, "cols", step)
     total, src, tgt, *strips = lax.optimization_barrier((total, src, tgt, *strips))
-    up, down = halo(src, tgt, strips)
-    above, below = shift(down, "rows", 1), shift(up, "rows", -1)
+    to_pair, to_next = halo(src, tgt, strips)
+    pair = exchange(to_pair, "rows", 0)
     for at, step in enumerate(powers("rows")):
-        total = total + swap(total, "rows", step)
+        total = total + swap(total, "rows", 2 * step - 1)
         if at == 0:
-            total, above, below = lax.optimization_barrier((total, above, below))
-    source, target = sinkhorn(src, tgt, above, below, strips)
+            total, pair, to_next = lax.optimization_barrier((total, pair, to_next))
+    following = exchange(to_next, "rows", 1)
+    source, target = sinkhorn(src, tgt, pair, following, strips)
     other = swap(total, "maps", 1)
     first, second, output, source, target = finish(total, other, source, target, cells, hid, feat)
     return first, second, output.reshape(hid), source, target

time: 41 us -> 38.3 us (0.934)
  starting transfers between devices: 14.1 us -> 9.05 us
  waiting for transfers between devices: 9.28 us -> 11.4 us
    ppermute x6, starting transfers between devices: 9.3 us -> 6.74 us  [swap(): lax.ppermute(value, axis, [(i, i ^ step) for i in range(lax.axis_size(axi...]
    ppermute x2, starting transfers between devices: 4.78 us -> 2.31 us  [exchange(): return lax.ppermute(value, axis, pairs)]
    ppermute x6, waiting for transfers between devices: 9.27 us -> 11.4 us  [swap(): lax.ppermute(value, axis, [(i, i ^ step) for i in range(lax.axis_size(axi...]
  transfers between devices with their start and end apart: 8 -> 8, of which waited for: 5 -> 5; matrix products, arithmetic and copies ran while one was open for 0% -> 0% of each run, Pallas kernels for 4% -> 5%
where the time goes in v3:
time: 38.3 us; the launch traced here: 38 us
  Pallas kernels  16.7 us (44%)
  waiting for transfers between devices  11.4 us (30%)
  starting transfers between devices  9.05 us (24%)
  between operations  0.75 us (2%)
    pallas_call x1, Pallas kernels, net(): pl.pallas_call(functools.partial(net_kernel, sides), out_shape=[vmem(hid...  14.1 us
    ppermute x6, waiting for transfers between devices, swap(): lax.ppermute(value, axis, [(i, i ^ step) for i in range(lax.axis_size(axi...  11.4 us
    ppermute x6, starting transfers between devices, swap(): lax.ppermute(value, axis, [(i, i ^ step) for i in range(lax.axis_size(axi...  6.74 us
    ppermute x2, starting transfers between devices, exchange(): return lax.ppermute(value, axis, pairs)  2.31 us
    pallas_call x1, Pallas kernels, sinkhorn(): pl.pallas_call(sinkhorn_kernel, out_shape=[vmem(rows, cols)] * 2, compile...  1.76 us
  transfers between devices with their start and end apart: 8, of which 5 were waited for; matrix products, arithmetic and copies ran while one was open for 0% of the time, Pallas kernels for 5%

profile of v3, /device:TPU:0, one launch (start us, length us, event | category | flops | bytes accessed | tf_op | source)
XLA Modules:
  0.0 38.0 jit_solution(6164618402806935777)
XLA Ops:
  0.6 0.0 copy-start.2
  0.6 14.1 %net.1 = (f32[80,128]{1,0:T(8,128)S(1)}, f32[80,128]{1,0:T(8,128)S(1)}, f32[128,128]{1,0:T(8,128)S(1)}, f32[128,128]{1,0:T(8,128)S(1)}, bf16[128,128]{1,0:T(8,128)(2,1)S(1)}) custom-call(bf16[1,16,128,128]{3,2,1,0:T(8,128)(2,1)} %refs_0_.1, bf16[1,128,128]{2,1,0:T(8,128)(2,1)} %refs_1_.1, bf16[1,128,128]{2,1,0:T(8,128)(2,1)} %refs_2_.1, s32[128,128]{1,0:T(8,128)} %refs_3_.1, ...), custom_call_target="tpu_custom_call" | custom-call | tf_op jit(solution)/shard_map/net/pallas_call | solution.py:185
  14.8 0.0 copy-start
  14.8 0.5 %collective-permute-start = (f32[80,128]{1,0:T(8,128)S(1)}, f32[80,128]{1,0:T(8,128)S(1)}, u32[]{:S(2)}, u32[]{:S(2)}) collective-permute-start(f32[80,128]{1,0:T(8,128)S(1)} %get-tuple-element.27), channel_id=1, source_target_pairs={{0,1},{1,0},{2,3},{3,2},{4,5},{5,4},{6,7},{7,6},{8,9},{9,8},{10,11... | collective-permute-start | bytes 122888 | tf_op jit(solution)/shard_map/ppermute | solution.py:410
  15.3 0.9 %collective-permute-done = f32[80,128]{1,0:T(8,128)S(1)} collective-permute-done((f32[80,128]{1,0:T(8,128)S(1)}, f32[80,128]{1,0:T(8,128)S(1)}, u32[]{:S(2)}, u32[]{:S(2)}) %collective-permute-start) | collective-permute-done | bytes 40992 | tf_op jit(solution)/shard_map/ppermute | solution.py:410
  16.2 0.0 copy-start.1
  16.2 2.9 %collective-permute-start.1 = (f32[80,128]{1,0:T(8,128)S(1)}, f32[80,128]{1,0:T(8,128)S(1)}, u32[]{:S(2)}, u32[]{:S(2)}) collective-permute-start(f32[80,128]{1,0:T(8,128)S(1)} %add.12), channel_id=1, source_target_pairs={{0,2},{2,0},{1,3},{3,1},{4,6},{6,4},{5,7},{7,5},{8,10},{10,8},{9,1... | collective-permute-start | bytes 122888 | tf_op jit(solution)/shard_map/ppermute | solution.py:410
  19.1 0.1 collective-permute-start.2
  19.2 1.9 %collective-permute-done.1 = f32[80,128]{1,0:T(8,128)S(1)} collective-permute-done((f32[80,128]{1,0:T(8,128)S(1)}, f32[80,128]{1,0:T(8,128)S(1)}, u32[]{:S(2)}, u32[]{:S(2)}) %collective-permute-start.1) | collective-permute-done | bytes 40992 | tf_op jit(solution)/shard_map/ppermute | solution.py:410
  21.1 1.9 %collective-permute-done.2.refs_0_ = bf16[128,128]{1,0:T(8,128)(2,1)S(1)} collective-permute-done((bf16[128,128]{1,0:T(8,128)(2,1)S(1)}, bf16[128,128]{1,0:T(8,128)(2,1)S(1)}, u32[]{:S(2)}, u32[]{:S(2)}) %collective-permute-start.2) | collective-permute-done | bytes 32800 | tf_op jit(solution)/shard_map/ppermute | solution.py:410
  23.0 0.1 halo.1
  23.1 1.6 %collective-permute-start.4 = (bf16[128,256]{1,0:T(8,128)(2,1)S(1)}, bf16[128,256]{1,0:T(8,128)(2,1)S(1)}, u32[]{:S(2)}, u32[]{:S(2)}) collective-permute-start(bf16[128,256]{1,0:T(8,128)(2,1)S(1)} %get-tuple-element.35), channel_id=1, source_target_pairs={{0,4},{4,0},{8,12},{12,8},{1,5},{5,1},{9,13},{13,9},{2,6},{6,2},{1... | collective-permute-start | bytes 196616 | tf_op jit(solution)/shard_map/ppermute | solution.py:422
  24.8 0.4 %collective-permute-start.3 = (f32[80,128]{1,0:T(8,128)S(1)}, f32[80,128]{1,0:T(8,128)S(1)}, u32[]{:S(2)}, u32[]{:S(2)}) collective-permute-start(f32[80,128]{1,0:T(8,128)S(1)} %add.13), channel_id=1, source_target_pairs={{0,4},{4,0},{8,12},{12,8},{1,5},{5,1},{9,13},{13,9},{2,6},{6,2},{1... | collective-permute-start | bytes 122888 | tf_op jit(solution)/shard_map/ppermute | solution.py:410
  25.2 3.6 %collective-permute-done.3 = f32[80,128]{1,0:T(8,128)S(1)} collective-permute-done((f32[80,128]{1,0:T(8,128)S(1)}, f32[80,128]{1,0:T(8,128)S(1)}, u32[]{:S(2)}, u32[]{:S(2)}) %collective-permute-start.3) | collective-permute-done | bytes 40992 | tf_op jit(solution)/shard_map/ppermute | solution.py:410
  28.8 0.0 collective-permute-done.4.pair_ref
  28.8 0.0 copy-start.3
  28.8 0.7 %collective-permute-start.7 = (bf16[128,256]{1,0:T(8,128)(2,1)S(1)}, bf16[128,256]{1,0:T(8,128)(2,1)S(1)}, u32[]{:S(2)}, u32[]{:S(2)}) collective-permute-start(bf16[128,256]{1,0:T(8,128)(2,1)S(1)} %get-tuple-element.39), channel_id=1, source_target_pairs={{4,8},{8,4},{5,9},{9,5},{6,10},{10,6},{7,11},{11,7},{20,24},{24,20... | collective-permute-start | bytes 196616 | tf_op jit(solution)/shard_map/ppermute | solution.py:422
  29.5 2.8 %collective-permute-start.5 = (f32[80,128]{1,0:T(8,128)S(1)}, f32[80,128]{1,0:T(8,128)S(1)}, u32[]{:S(2)}, u32[]{:S(2)}) collective-permute-start(f32[80,128]{1,0:T(8,128)S(1)} %add.14), channel_id=1, source_target_pairs={{0,12},{4,8},{8,4},{12,0},{1,13},{5,9},{9,5},{13,1},{2,14},{6,10},... | collective-permute-start | bytes 122888 | tf_op jit(solution)/shard_map/ppermute | solution.py:410
  32.2 3.2 %collective-permute-done.5 = f32[80,128]{1,0:T(8,128)S(1)} collective-permute-done((f32[80,128]{1,0:T(8,128)S(1)}, f32[80,128]{1,0:T(8,128)S(1)}, u32[]{:S(2)}, u32[]{:S(2)}) %collective-permute-start.5) | collective-permute-done | bytes 40992 | tf_op jit(solution)/shard_map/ppermute | solution.py:410
  35.4 0.0 collective-permute-start.6
  35.4 0.0 collective-permute-done.7.next_ref
  35.5 0.0 copy-done.2
  35.5 0.0 copy-done
  35.5 0.0 copy-done.1
  35.5 0.0 copy-done.3
  35.5 1.8 %sinkhorn.1 = (f32[128,128]{1,0:T(8,128)S(1)}, f32[128,128]{1,0:T(8,128)S(1)}) custom-call(f32[128,128]{1,0:T(8,128)S(1)} %get-tuple-element.32.src_ref, f32[128,128]{1,0:T(8,128)S(1)} %get-tuple-element.33.tgt_ref, bf16[128,256]{1,0:T(8,128)(2,1)S(1)} %collective-permute-done.4.pair_ref, bf16[128,256]{1,0:T(8,128)(2,1)S(1)} %collective-permute-done.7.next_ref, ...), custom_call_target="tpu_custom_call" | custom-call | flops 2000000000 | bytes 1000000 | tf_op jit(solution)/shard_map/sinkhorn/pallas_call | solution.py:365
  37.3 0.0 collective-permute-done.6.other_ref
  37.3 0.7 %finish.1 = (f32[16,128]{1,0:T(8,128)}, f32[128,128]{1,0:T(8,128)}, f32[1,128]{1,0:T(1,128)}, f32[1,128,128]{2,1,0:T(8,128)}, f32[1,128,128]{2,1,0:T(8,128)}) custom-call(f32[80,128]{1,0:T(8,128)S(1)} %add.15.mine_ref, f32[80,128]{1,0:T(8,128)S(1)} %collective-permute-done.6.other_ref, f32[128,128]{1,0:T(8,128)S(1)} %get-tuple-element.40.source_ref, ...), custom_call_target="tpu_custom_call" | custom-call | tf_op jit(solution)/shard_map/finish/pallas_call | solution.py:395
  (4 shorter events, 0.0 us)
Async XLA Ops:
  0.6 34.8 %copy-start.2 = (bf16[2,256,256]{2,1,0:T(8,128)(2,1)S(1)}, bf16[2,256,256]{2,1,0:T(8,128)(2,1)}, u32[]{:S(2)}) copy-start(bf16[2,256,256]{2,1,0:T(8,128)(2,1)} %constant.9.clone.bcol_ref) | copy-start | bytes 786436
  14.8 20.7 %copy-start = (bf16[2,224,272]{2,1,0:T(8,128)(2,1)S(1)}, bf16[2,224,272]{2,1,0:T(8,128)(2,1)}, u32[]{:S(2)}) copy-start(bf16[2,224,272]{2,1,0:T(8,128)(2,1)} %constant.8.clone.brow_ref) | copy-start | bytes 731140
  14.8 1.4 %collective-permute-start = (f32[80,128]{1,0:T(8,128)S(1)}, f32[80,128]{1,0:T(8,128)S(1)}, u32[]{:S(2)}, u32[]{:S(2)}) collective-permute-start(f32[80,128]{1,0:T(8,128)S(1)} %get-tuple-element.27), channel_id=1, source_target_pairs={{0,1},{1,0},{2,3},{3,2},{4,5},{5,4},{6,7},{7,6},{8,9},{9,8},{10,11... | collective-permute-start | bytes 122888 | tf_op jit(solution)/shard_map/ppermute | solution.py:410
  16.2 19.3 %copy-start.1 = (f32[2,272,128]{2,1,0:T(8,128)S(1)}, f32[2,272,128]{2,1,0:T(8,128)}, u32[]{:S(2)}) copy-start(f32[2,272,128]{2,1,0:T(8,128)} %constant.10.clone.krow_ref) | copy-start | bytes 835588
  16.2 4.9 %collective-permute-start.1 = (f32[80,128]{1,0:T(8,128)S(1)}, f32[80,128]{1,0:T(8,128)S(1)}, u32[]{:S(2)}, u32[]{:S(2)}) collective-permute-start(f32[80,128]{1,0:T(8,128)S(1)} %add.12), channel_id=1, source_target_pairs={{0,2},{2,0},{1,3},{3,1},{4,6},{6,4},{5,7},{7,5},{8,10},{10,8},{9,1... | collective-permute-start | bytes 122888 | tf_op jit(solution)/shard_map/ppermute | solution.py:410
  19.1 3.9 %collective-permute-start.2 = (bf16[128,128]{1,0:T(8,128)(2,1)S(1)}, bf16[128,128]{1,0:T(8,128)(2,1)S(1)}, u32[]{:S(2)}, u32[]{:S(2)}) collective-permute-start(bf16[128,128]{1,0:T(8,128)(2,1)S(1)} %get-tuple-element.30), channel_id=1, source_target_pairs={{0,2},{2,0},{1,3},{3,1},{4,6},{6,4},{5,7},{7,5},{8,10},{10,8},{9,1... | collective-permute-start | bytes 98312 | tf_op jit(solution)/shard_map/ppermute | solution.py:410
  23.1 5.7 %collective-permute-start.4 = (bf16[128,256]{1,0:T(8,128)(2,1)S(1)}, bf16[128,256]{1,0:T(8,128)(2,1)S(1)}, u32[]{:S(2)}, u32[]{:S(2)}) collective-permute-start(bf16[128,256]{1,0:T(8,128)(2,1)S(1)} %get-tuple-element.35), channel_id=1, source_target_pairs={{0,4},{4,0},{8,12},{12,8},{1,5},{5,1},{9,13},{13,9},{2,6},{6,2},{1... | collective-permute-start | bytes 196616 | tf_op jit(solution)/shard_map/ppermute | solution.py:422
  24.8 4.0 %collective-permute-start.3 = (f32[80,128]{1,0:T(8,128)S(1)}, f32[80,128]{1,0:T(8,128)S(1)}, u32[]{:S(2)}, u32[]{:S(2)}) collective-permute-start(f32[80,128]{1,0:T(8,128)S(1)} %add.13), channel_id=1, source_target_pairs={{0,4},{4,0},{8,12},{12,8},{1,5},{5,1},{9,13},{13,9},{2,6},{6,2},{1... | collective-permute-start | bytes 122888 | tf_op jit(solution)/shard_map/ppermute | solution.py:410
  28.8 6.7 %copy-start.3 = (f32[8,256]{1,0:T(8,128)S(1)}, f32[8,256]{1,0:T(8,128)}, u32[]{:S(2)}) copy-start(f32[8,256]{1,0:T(8,128)} %constant.11.clone.kcol_ref) | copy-start | bytes 24580
  28.8 6.7 %collective-permute-start.7 = (bf16[128,256]{1,0:T(8,128)(2,1)S(1)}, bf16[128,256]{1,0:T(8,128)(2,1)S(1)}, u32[]{:S(2)}, u32[]{:S(2)}) collective-permute-start(bf16[128,256]{1,0:T(8,128)(2,1)S(1)} %get-tuple-element.39), channel_id=1, source_target_pairs={{4,8},{8,4},{5,9},{9,5},{6,10},{10,6},{7,11},{11,7},{20,24},{24,20... | collective-permute-start | bytes 196616 | tf_op jit(solution)/shard_map/ppermute | solution.py:422
  29.5 6.0 %collective-permute-start.5 = (f32[80,128]{1,0:T(8,128)S(1)}, f32[80,128]{1,0:T(8,128)S(1)}, u32[]{:S(2)}, u32[]{:S(2)}) collective-permute-start(f32[80,128]{1,0:T(8,128)S(1)} %add.14), channel_id=1, source_target_pairs={{0,12},{4,8},{8,4},{12,0},{1,13},{5,9},{9,5},{13,1},{2,14},{6,10},... | collective-permute-start | bytes 122888 | tf_op jit(solution)/shard_map/ppermute | solution.py:410
  35.4 1.8 %collective-permute-start.6 = (f32[80,128]{1,0:T(8,128)S(1)}, f32[80,128]{1,0:T(8,128)S(1)}, u32[]{:S(2)}, u32[]{:S(2)}) collective-permute-start(f32[80,128]{1,0:T(8,128)S(1)} %add.15.mine_ref), channel_id=1, source_target_pairs={{0,1},{1,0},{2,3},{3,2},{4,5},{5,4},{6,7},{7,6},{8,9},{9,8},{10,11... | collective-permute-start | bytes 122888 | tf_op jit(solution)/shard_map/ppermute | solution.py:410

commit v4 on v3

--- a/solution.py
+++ b/solution.py
@@ -163,7 +163,7 @@
         if sides == 1:
             strips = [jnp.where(lax.axis_index("cols") == 0, right, left)]
         for ref, strip in zip(strip_outs, strips):
-            ref[...] = strip.astype(BF)
+            ref[...] = strip
 
 
 def vmem(*shape, dtype=F32):
@@ -186,7 +186,7 @@
         functools.partial(net_kernel, sides),
         out_shape=[vmem(hid // 2 + feat, 128)] * 2
         + [vmem(rows, cols)] * 2
-        + [vmem(rows, cols, dtype=BF)] * sides,
+        + [vmem(rows, cols)] * sides,
         scratch_shapes=[vmem(hid, wide, dtype=BF)] * 3
         + [vmem(hid, wide)] * 6
         + [vmem(hid, wide, dtype=BF)] * 3

time: 38.3 us -> 37.2 us (0.971)
  waiting for transfers between devices: 11.4 us -> 9.61 us
  starting transfers between devices: 9.05 us -> 9.84 us
    ppermute x6, waiting for transfers between devices: 11.4 us -> 9.6 us  [swap(): lax.ppermute(value, axis, [(i, i ^ step) for i in range(lax.axis_size(axi...]
    ppermute x6, starting transfers between devices: 6.74 us -> 7.53 us  [swap(): lax.ppermute(value, axis, [(i, i ^ step) for i in range(lax.axis_size(axi...]
  transfers between devices with their start and end apart: 8 -> 8, of which waited for: 5 -> 3; matrix products, arithmetic and copies ran while one was open for 0% -> 0% of each run, Pallas kernels for 5% -> 5%
where the time goes in v4:
time: 37.2 us; the launch traced here: 36.9 us
  Pallas kernels  16.7 us (45%)
  starting transfers between devices  9.84 us (26%)
  waiting for transfers between devices  9.61 us (26%)
  between operations  0.76 us (2%)
    pallas_call x1, Pallas kernels, net(): pl.pallas_call(functools.partial(net_kernel, sides), out_shape=[vmem(hid...  14.1 us
    ppermute x6, waiting for transfers between devices, swap(): lax.ppermute(value, axis, [(i, i ^ step) for i in range(lax.axis_size(axi...  9.6 us
    ppermute x6, starting transfers between devices, swap(): lax.ppermute(value, axis, [(i, i ^ step) for i in range(lax.axis_size(axi...  7.53 us
    ppermute x2, starting transfers between devices, exchange(): return lax.ppermute(value, axis, pairs)  2.31 us
    pallas_call x1, Pallas kernels, sinkhorn(): pl.pallas_call(sinkhorn_kernel, out_shape=[vmem(rows, cols)] * 2, compile...  1.75 us
  transfers between devices with their start and end apart: 8, of which 3 were waited for; matrix products, arithmetic and copies ran while one was open for 0% of the time, Pallas kernels for 5%

profile of v4, /device:TPU:0, one launch (start us, length us, event | category | flops | bytes accessed | tf_op | source)
XLA Modules:
  0.0 36.9 jit_solution(12679218167653584486)
XLA Ops:
  0.6 0.0 copy-start.2
  0.6 14.1 %net.1 = (f32[80,128]{1,0:T(8,128)S(1)}, f32[80,128]{1,0:T(8,128)S(1)}, f32[128,128]{1,0:T(8,128)S(1)}, f32[128,128]{1,0:T(8,128)S(1)}, f32[128,128]{1,0:T(8,128)S(1)}) custom-call(bf16[1,16,128,128]{3,2,1,0:T(8,128)(2,1)} %refs_0_.1, bf16[1,128,128]{2,1,0:T(8,128)(2,1)} %refs_1_.1, bf16[1,128,128]{2,1,0:T(8,128)(2,1)} %refs_2_.1, s32[128,128]{1,0:T(8,128)} %refs_3_.1, ...), custom_call_target="tpu_custom_call" | custom-call | tf_op jit(solution)/shard_map/net/pallas_call | solution.py:185
  14.8 0.5 %collective-permute-start = (f32[80,128]{1,0:T(8,128)S(1)}, f32[80,128]{1,0:T(8,128)S(1)}, u32[]{:S(2)}, u32[]{:S(2)}) collective-permute-start(f32[80,128]{1,0:T(8,128)S(1)} %get-tuple-element.27), channel_id=1, source_target_pairs={{0,1},{1,0},{2,3},{3,2},{4,5},{5,4},{6,7},{7,6},{8,9},{9,8},{10,11... | collective-permute-start | bytes 122888 | tf_op jit(solution)/shard_map/ppermute | solution.py:410
  15.3 2.6 %collective-permute-start.2 = (f32[128,128]{1,0:T(8,128)S(1)}, f32[128,128]{1,0:T(8,128)S(1)}, u32[]{:S(2)}, u32[]{:S(2)}) collective-permute-start(f32[128,128]{1,0:T(8,128)S(1)} %get-tuple-element.30), channel_id=1, source_target_pairs={{0,2},{2,0},{1,3},{3,1},{4,6},{6,4},{5,7},{7,5},{8,10},{10,8},{9,1... | collective-permute-start | bytes 196616 | tf_op jit(solution)/shard_map/ppermute | solution.py:410
  17.9 0.0 collective-permute-done
  17.9 0.0 copy-start
  17.9 0.0 copy-start.1
  17.9 1.2 %collective-permute-start.1 = (f32[80,128]{1,0:T(8,128)S(1)}, f32[80,128]{1,0:T(8,128)S(1)}, u32[]{:S(2)}, u32[]{:S(2)}) collective-permute-start(f32[80,128]{1,0:T(8,128)S(1)} %add.12), channel_id=1, source_target_pairs={{0,2},{2,0},{1,3},{3,1},{4,6},{6,4},{5,7},{7,5},{8,10},{10,8},{9,1... | collective-permute-start | bytes 122888 | tf_op jit(solution)/shard_map/ppermute | solution.py:410
  19.1 2.9 %collective-permute-done.1 = f32[80,128]{1,0:T(8,128)S(1)} collective-permute-done((f32[80,128]{1,0:T(8,128)S(1)}, f32[80,128]{1,0:T(8,128)S(1)}, u32[]{:S(2)}, u32[]{:S(2)}) %collective-permute-start.1) | collective-permute-done | bytes 40992 | tf_op jit(solution)/shard_map/ppermute | solution.py:410
  22.0 0.0 collective-permute-done.2.refs_0_
  22.0 0.1 halo.1
  22.1 1.6 %collective-permute-start.4 = (bf16[128,256]{1,0:T(8,128)(2,1)S(1)}, bf16[128,256]{1,0:T(8,128)(2,1)S(1)}, u32[]{:S(2)}, u32[]{:S(2)}) collective-permute-start(bf16[128,256]{1,0:T(8,128)(2,1)S(1)} %get-tuple-element.35), channel_id=1, source_target_pairs={{0,4},{4,0},{8,12},{12,8},{1,5},{5,1},{9,13},{13,9},{2,6},{6,2},{1... | collective-permute-start | bytes 196616 | tf_op jit(solution)/shard_map/ppermute | solution.py:422
  23.7 0.4 %collective-permute-start.3 = (f32[80,128]{1,0:T(8,128)S(1)}, f32[80,128]{1,0:T(8,128)S(1)}, u32[]{:S(2)}, u32[]{:S(2)}) collective-permute-start(f32[80,128]{1,0:T(8,128)S(1)} %add.13), channel_id=1, source_target_pairs={{0,4},{4,0},{8,12},{12,8},{1,5},{5,1},{9,13},{13,9},{2,6},{6,2},{1... | collective-permute-start | bytes 122888 | tf_op jit(solution)/shard_map/ppermute | solution.py:410
  24.2 3.6 %collective-permute-done.3 = f32[80,128]{1,0:T(8,128)S(1)} collective-permute-done((f32[80,128]{1,0:T(8,128)S(1)}, f32[80,128]{1,0:T(8,128)S(1)}, u32[]{:S(2)}, u32[]{:S(2)}) %collective-permute-start.3) | collective-permute-done | bytes 40992 | tf_op jit(solution)/shard_map/ppermute | solution.py:410
  27.7 0.0 collective-permute-done.4.pair_ref
  27.7 0.0 copy-start.3
  27.7 0.7 %collective-permute-start.7 = (bf16[128,256]{1,0:T(8,128)(2,1)S(1)}, bf16[128,256]{1,0:T(8,128)(2,1)S(1)}, u32[]{:S(2)}, u32[]{:S(2)}) collective-permute-start(bf16[128,256]{1,0:T(8,128)(2,1)S(1)} %get-tuple-element.39), channel_id=1, source_target_pairs={{4,8},{8,4},{5,9},{9,5},{6,10},{10,6},{7,11},{11,7},{20,24},{24,20... | collective-permute-start | bytes 196616 | tf_op jit(solution)/shard_map/ppermute | solution.py:422
  28.4 2.8 %collective-permute-start.5 = (f32[80,128]{1,0:T(8,128)S(1)}, f32[80,128]{1,0:T(8,128)S(1)}, u32[]{:S(2)}, u32[]{:S(2)}) collective-permute-start(f32[80,128]{1,0:T(8,128)S(1)} %add.14), channel_id=1, source_target_pairs={{0,12},{4,8},{8,4},{12,0},{1,13},{5,9},{9,5},{13,1},{2,14},{6,10},... | collective-permute-start | bytes 122888 | tf_op jit(solution)/shard_map/ppermute | solution.py:410
  31.2 3.2 %collective-permute-done.5 = f32[80,128]{1,0:T(8,128)S(1)} collective-permute-done((f32[80,128]{1,0:T(8,128)S(1)}, f32[80,128]{1,0:T(8,128)S(1)}, u32[]{:S(2)}, u32[]{:S(2)}) %collective-permute-start.5) | collective-permute-done | bytes 40992 | tf_op jit(solution)/shard_map/ppermute | solution.py:410
  34.4 0.0 collective-permute-start.6
  34.4 0.0 collective-permute-done.7.next_ref
  34.4 0.0 copy-done.2
  34.4 0.0 copy-done
  34.4 0.0 copy-done.1
  34.4 0.0 copy-done.3
  34.5 1.8 %sinkhorn.1 = (f32[128,128]{1,0:T(8,128)S(1)}, f32[128,128]{1,0:T(8,128)S(1)}) custom-call(f32[128,128]{1,0:T(8,128)S(1)} %get-tuple-element.32.src_ref, f32[128,128]{1,0:T(8,128)S(1)} %get-tuple-element.33.tgt_ref, bf16[128,256]{1,0:T(8,128)(2,1)S(1)} %collective-permute-done.4.pair_ref, bf16[128,256]{1,0:T(8,128)(2,1)S(1)} %collective-permute-done.7.next_ref, ...), custom_call_target="tpu_custom_call" | custom-call | flops 2000000000 | bytes 1000000 | tf_op jit(solution)/shard_map/sinkhorn/pallas_call | solution.py:365
  36.2 0.0 collective-permute-done.6.other_ref
  36.2 0.7 %finish.1 = (f32[16,128]{1,0:T(8,128)}, f32[128,128]{1,0:T(8,128)}, f32[1,128]{1,0:T(1,128)}, f32[1,128,128]{2,1,0:T(8,128)}, f32[1,128,128]{2,1,0:T(8,128)}) custom-call(f32[80,128]{1,0:T(8,128)S(1)} %add.15.mine_ref, f32[80,128]{1,0:T(8,128)S(1)} %collective-permute-done.6.other_ref, f32[128,128]{1,0:T(8,128)S(1)} %get-tuple-element.40.source_ref, ...), custom_call_target="tpu_custom_call" | custom-call | tf_op jit(solution)/shard_map/finish/pallas_call | solution.py:395
  (4 shorter events, 0.0 us)
Async XLA Ops:
  0.6 33.8 %copy-start.2 = (bf16[2,256,256]{2,1,0:T(8,128)(2,1)S(1)}, bf16[2,256,256]{2,1,0:T(8,128)(2,1)}, u32[]{:S(2)}) copy-start(bf16[2,256,256]{2,1,0:T(8,128)(2,1)} %constant.9.clone.bcol_ref) | copy-start | bytes 786436
  14.8 3.1 %collective-permute-start = (f32[80,128]{1,0:T(8,128)S(1)}, f32[80,128]{1,0:T(8,128)S(1)}, u32[]{:S(2)}, u32[]{:S(2)}) collective-permute-start(f32[80,128]{1,0:T(8,128)S(1)} %get-tuple-element.27), channel_id=1, source_target_pairs={{0,1},{1,0},{2,3},{3,2},{4,5},{5,4},{6,7},{7,6},{8,9},{9,8},{10,11... | collective-permute-start | bytes 122888 | tf_op jit(solution)/shard_map/ppermute | solution.py:410
  15.3 6.7 %collective-permute-start.2 = (f32[128,128]{1,0:T(8,128)S(1)}, f32[128,128]{1,0:T(8,128)S(1)}, u32[]{:S(2)}, u32[]{:S(2)}) collective-permute-start(f32[128,128]{1,0:T(8,128)S(1)} %get-tuple-element.30), channel_id=1, source_target_pairs={{0,2},{2,0},{1,3},{3,1},{4,6},{6,4},{5,7},{7,5},{8,10},{10,8},{9,1... | collective-permute-start | bytes 196616 | tf_op jit(solution)/shard_map/ppermute | solution.py:410
  17.9 16.6 %copy-start = (bf16[2,224,272]{2,1,0:T(8,128)(2,1)S(1)}, bf16[2,224,272]{2,1,0:T(8,128)(2,1)}, u32[]{:S(2)}) copy-start(bf16[2,224,272]{2,1,0:T(8,128)(2,1)} %constant.8.clone.brow_ref) | copy-start | bytes 731140
  17.9 16.6 %copy-start.1 = (f32[2,272,128]{2,1,0:T(8,128)S(1)}, f32[2,272,128]{2,1,0:T(8,128)}, u32[]{:S(2)}) copy-start(f32[2,272,128]{2,1,0:T(8,128)} %constant.10.clone.krow_ref) | copy-start | bytes 835588
  17.9 4.1 %collective-permute-start.1 = (f32[80,128]{1,0:T(8,128)S(1)}, f32[80,128]{1,0:T(8,128)S(1)}, u32[]{:S(2)}, u32[]{:S(2)}) collective-permute-start(f32[80,128]{1,0:T(8,128)S(1)} %add.12), channel_id=1, source_target_pairs={{0,2},{2,0},{1,3},{3,1},{4,6},{6,4},{5,7},{7,5},{8,10},{10,8},{9,1... | collective-permute-start | bytes 122888 | tf_op jit(solution)/shard_map/ppermute | solution.py:410
  22.1 5.7 %collective-permute-start.4 = (bf16[128,256]{1,0:T(8,128)(2,1)S(1)}, bf16[128,256]{1,0:T(8,128)(2,1)S(1)}, u32[]{:S(2)}, u32[]{:S(2)}) collective-permute-start(bf16[128,256]{1,0:T(8,128)(2,1)S(1)} %get-tuple-element.35), channel_id=1, source_target_pairs={{0,4},{4,0},{8,12},{12,8},{1,5},{5,1},{9,13},{13,9},{2,6},{6,2},{1... | collective-permute-start | bytes 196616 | tf_op jit(solution)/shard_map/ppermute | solution.py:422
  23.7 4.0 %collective-permute-start.3 = (f32[80,128]{1,0:T(8,128)S(1)}, f32[80,128]{1,0:T(8,128)S(1)}, u32[]{:S(2)}, u32[]{:S(2)}) collective-permute-start(f32[80,128]{1,0:T(8,128)S(1)} %add.13), channel_id=1, source_target_pairs={{0,4},{4,0},{8,12},{12,8},{1,5},{5,1},{9,13},{13,9},{2,6},{6,2},{1... | collective-permute-start | bytes 122888 | tf_op jit(solution)/shard_map/ppermute | solution.py:410
  27.7 6.7 %copy-start.3 = (f32[8,256]{1,0:T(8,128)S(1)}, f32[8,256]{1,0:T(8,128)}, u32[]{:S(2)}) copy-start(f32[8,256]{1,0:T(8,128)} %constant.11.clone.kcol_ref) | copy-start | bytes 24580
  27.7 6.7 %collective-permute-start.7 = (bf16[128,256]{1,0:T(8,128)(2,1)S(1)}, bf16[128,256]{1,0:T(8,128)(2,1)S(1)}, u32[]{:S(2)}, u32[]{:S(2)}) collective-permute-start(bf16[128,256]{1,0:T(8,128)(2,1)S(1)} %get-tuple-element.39), channel_id=1, source_target_pairs={{4,8},{8,4},{5,9},{9,5},{6,10},{10,6},{7,11},{11,7},{20,24},{24,20... | collective-permute-start | bytes 196616 | tf_op jit(solution)/shard_map/ppermute | solution.py:422
  28.4 6.0 %collective-permute-start.5 = (f32[80,128]{1,0:T(8,128)S(1)}, f32[80,128]{1,0:T(8,128)S(1)}, u32[]{:S(2)}, u32[]{:S(2)}) collective-permute-start(f32[80,128]{1,0:T(8,128)S(1)} %add.14), channel_id=1, source_target_pairs={{0,12},{4,8},{8,4},{12,0},{1,13},{5,9},{9,5},{13,1},{2,14},{6,10},... | collective-permute-start | bytes 122888 | tf_op jit(solution)/shard_map/ppermute | solution.py:410
  34.4 1.8 %collective-permute-start.6 = (f32[80,128]{1,0:T(8,128)S(1)}, f32[80,128]{1,0:T(8,128)S(1)}, u32[]{:S(2)}, u32[]{:S(2)}) collective-permute-start(f32[80,128]{1,0:T(8,128)S(1)} %add.15.mine_ref), channel_id=1, source_target_pairs={{0,1},{1,0},{2,3},{3,2},{4,5},{5,4},{6,7},{7,6},{8,9},{9,8},{10,11... | collective-permute-start | bytes 122888 | tf_op jit(solution)/shard_map/ppermute | solution.py:410

commit v5 on v4

--- a/solution.py
+++ b/solution.py
@@ -443,7 +443,6 @@
         strips = [shift(strips[0], "cols", 1), shift(strips[1], "cols", -1)]
     for step in powers("cols"):
         total = total + swap(total, "cols", step)
-    total, src, tgt, *strips = lax.optimization_barrier((total, src, tgt, *strips))
     to_pair, to_next = halo(src, tgt, strips)
     pair = exchange(to_pair, "rows", 0)
     for at, step in enumerate(powers("rows")):

time: 37.2 us -> 36.6 us (0.984)
  waiting for transfers between devices: 9.61 us -> 7.5 us
  starting transfers between devices: 9.84 us -> 11.2 us
    ppermute x6, waiting for transfers between devices: 9.6 us -> 7.49 us  [swap(): lax.ppermute(value, axis, [(i, i ^ step) for i in range(lax.axis_size(axi...]
    ppermute x6, starting transfers between devices: 7.53 us -> 8.4 us  [swap(): lax.ppermute(value, axis, [(i, i ^ step) for i in range(lax.axis_size(axi...]
    ppermute x2, starting transfers between devices: 2.31 us -> 2.84 us  [exchange(): return lax.ppermute(value, axis, pairs)]
  transfers between devices with their start and end apart: 8 -> 8, of which waited for: 3 -> 5; matrix products, arithmetic and copies ran while one was open for 0% -> 0% of each run, Pallas kernels for 5% -> 5%
where the time goes in v5:
time: 36.6 us; the launch traced here: 36.2 us
  Pallas kernels  16.7 us (46%)
  starting transfers between devices  11.2 us (31%)
  waiting for transfers between devices  7.5 us (20%)
  between operations  0.75 us (2%)
    pallas_call x1, Pallas kernels, net(): pl.pallas_call(functools.partial(net_kernel, sides), out_shape=[vmem(hid...  14.1 us
    ppermute x6, starting transfers between devices, swap(): lax.ppermute(value, axis, [(i, i ^ step) for i in range(lax.axis_size(axi...  8.4 us
    ppermute x6, waiting for transfers between devices, swap(): lax.ppermute(value, axis, [(i, i ^ step) for i in range(lax.axis_size(axi...  7.49 us
    ppermute x2, starting transfers between devices, exchange(): return lax.ppermute(value, axis, pairs)  2.84 us
    pallas_call x1, Pallas kernels, sinkhorn(): pl.pallas_call(sinkhorn_kernel, out_shape=[vmem(rows, cols)] * 2, compile...  1.75 us
  transfers between devices with their start and end apart: 8, of which 5 were waited for; matrix products, arithmetic and copies ran while one was open for 0% of the time, Pallas kernels for 5%

profile of v5, /device:TPU:0, one launch (start us, length us, event | category | flops | bytes accessed | tf_op | source)
XLA Modules:
  0.0 36.2 jit_solution(12767237103286071317)
XLA Ops:
  0.6 0.0 copy-start.2
  0.6 14.1 %net.1 = (f32[80,128]{1,0:T(8,128)S(1)}, f32[80,128]{1,0:T(8,128)S(1)}, f32[128,128]{1,0:T(8,128)S(1)}, f32[128,128]{1,0:T(8,128)S(1)}, f32[128,128]{1,0:T(8,128)S(1)}) custom-call(bf16[1,16,128,128]{3,2,1,0:T(8,128)(2,1)} %refs_0_.1, bf16[1,128,128]{2,1,0:T(8,128)(2,1)} %refs_1_.1, bf16[1,128,128]{2,1,0:T(8,128)(2,1)} %refs_2_.1, s32[128,128]{1,0:T(8,128)} %refs_3_.1, ...), custom_call_target="tpu_custom_call" | custom-call | tf_op jit(solution)/shard_map/net/pallas_call | solution.py:185
  14.8 3.0 %collective-permute-start.3 = (f32[128,128]{1,0:T(8,128)S(1)}, f32[128,128]{1,0:T(8,128)S(1)}, u32[]{:S(2)}, u32[]{:S(2)}) collective-permute-start(f32[128,128]{1,0:T(8,128)S(1)} %get-tuple-element.26), channel_id=1, source_target_pairs={{0,2},{2,0},{1,3},{3,1},{4,6},{6,4},{5,7},{7,5},{8,10},{10,8},{9,1... | collective-permute-start | bytes 196616 | tf_op jit(solution)/shard_map/ppermute | solution.py:410
  17.8 0.0 collective-permute-start
  17.8 1.2 %collective-permute-done = f32[80,128]{1,0:T(8,128)S(1)} collective-permute-done((f32[80,128]{1,0:T(8,128)S(1)}, f32[80,128]{1,0:T(8,128)S(1)}, u32[]{:S(2)}, u32[]{:S(2)}) %collective-permute-start) | collective-permute-done | bytes 40992 | tf_op jit(solution)/shard_map/ppermute | solution.py:410
  19.0 0.0 copy-start
  19.0 0.1 collective-permute-start.1
  19.2 0.9 %collective-permute-done.3.refs_0_ = f32[128,128]{1,0:T(8,128)S(1)} collective-permute-done((f32[128,128]{1,0:T(8,128)S(1)}, f32[128,128]{1,0:T(8,128)S(1)}, u32[]{:S(2)}, u32[]{:S(2)}) %collective-permute-start.3) | collective-permute-done | bytes 65568 | tf_op jit(solution)/shard_map/ppermute | solution.py:410
  20.0 0.0 copy-start.1
  20.0 0.1 halo.1
  20.1 2.2 %collective-permute-start.4 = (bf16[128,256]{1,0:T(8,128)(2,1)S(1)}, bf16[128,256]{1,0:T(8,128)(2,1)S(1)}, u32[]{:S(2)}, u32[]{:S(2)}) collective-permute-start(bf16[128,256]{1,0:T(8,128)(2,1)S(1)} %get-tuple-element.27), channel_id=1, source_target_pairs={{0,4},{4,0},{8,12},{12,8},{1,5},{5,1},{9,13},{13,9},{2,6},{6,2},{1... | collective-permute-start | bytes 196616 | tf_op jit(solution)/shard_map/ppermute | solution.py:422
  22.3 0.8 %collective-permute-done.1 = f32[80,128]{1,0:T(8,128)S(1)} collective-permute-done((f32[80,128]{1,0:T(8,128)S(1)}, f32[80,128]{1,0:T(8,128)S(1)}, u32[]{:S(2)}, u32[]{:S(2)}) %collective-permute-start.1) | collective-permute-done | bytes 40992 | tf_op jit(solution)/shard_map/ppermute | solution.py:410
  23.1 1.6 %collective-permute-start.2 = (f32[80,128]{1,0:T(8,128)S(1)}, f32[80,128]{1,0:T(8,128)S(1)}, u32[]{:S(2)}, u32[]{:S(2)}) collective-permute-start(f32[80,128]{1,0:T(8,128)S(1)} %add.13), channel_id=1, source_target_pairs={{0,4},{4,0},{8,12},{12,8},{1,5},{5,1},{9,13},{13,9},{2,6},{6,2},{1... | collective-permute-start | bytes 122888 | tf_op jit(solution)/shard_map/ppermute | solution.py:410
  24.7 2.4 %collective-permute-done.2 = f32[80,128]{1,0:T(8,128)S(1)} collective-permute-done((f32[80,128]{1,0:T(8,128)S(1)}, f32[80,128]{1,0:T(8,128)S(1)}, u32[]{:S(2)}, u32[]{:S(2)}) %collective-permute-start.2) | collective-permute-done | bytes 40992 | tf_op jit(solution)/shard_map/ppermute | solution.py:410
  27.1 0.0 collective-permute-done.4.pair_ref
  27.1 0.0 copy-start.3
  27.1 0.7 %collective-permute-start.7 = (bf16[128,256]{1,0:T(8,128)(2,1)S(1)}, bf16[128,256]{1,0:T(8,128)(2,1)S(1)}, u32[]{:S(2)}, u32[]{:S(2)}) collective-permute-start(bf16[128,256]{1,0:T(8,128)(2,1)S(1)} %get-tuple-element.31), channel_id=1, source_target_pairs={{4,8},{8,4},{5,9},{9,5},{6,10},{10,6},{7,11},{11,7},{20,24},{24,20... | collective-permute-start | bytes 196616 | tf_op jit(solution)/shard_map/ppermute | solution.py:422
  27.8 3.7 %collective-permute-start.5 = (f32[80,128]{1,0:T(8,128)S(1)}, f32[80,128]{1,0:T(8,128)S(1)}, u32[]{:S(2)}, u32[]{:S(2)}) collective-permute-start(f32[80,128]{1,0:T(8,128)S(1)} %add.14), channel_id=1, source_target_pairs={{0,12},{4,8},{8,4},{12,0},{1,13},{5,9},{9,5},{13,1},{2,14},{6,10},... | collective-permute-start | bytes 122888 | tf_op jit(solution)/shard_map/ppermute | solution.py:410
  31.5 2.2 %collective-permute-done.5 = f32[80,128]{1,0:T(8,128)S(1)} collective-permute-done((f32[80,128]{1,0:T(8,128)S(1)}, f32[80,128]{1,0:T(8,128)S(1)}, u32[]{:S(2)}, u32[]{:S(2)}) %collective-permute-start.5) | collective-permute-done | bytes 40992 | tf_op jit(solution)/shard_map/ppermute | solution.py:410
  33.7 0.0 collective-permute-start.6
  33.7 0.0 collective-permute-done.7.next_ref
  33.7 0.0 copy-done.2
  33.7 0.0 copy-done
  33.7 0.0 copy-done.1
  33.7 0.0 copy-done.3
  33.7 1.8 %sinkhorn.1 = (f32[128,128]{1,0:T(8,128)S(1)}, f32[128,128]{1,0:T(8,128)S(1)}) custom-call(f32[128,128]{1,0:T(8,128)S(1)} %get-tuple-element.24.src_ref, f32[128,128]{1,0:T(8,128)S(1)} %get-tuple-element.25.tgt_ref, bf16[128,256]{1,0:T(8,128)(2,1)S(1)} %collective-permute-done.4.pair_ref, bf16[128,256]{1,0:T(8,128)(2,1)S(1)} %collective-permute-done.7.next_ref, ...), custom_call_target="tpu_custom_call" | custom-call | flops 2000000000 | bytes 1000000 | tf_op jit(solution)/shard_map/sinkhorn/pallas_call | solution.py:365
  35.5 0.0 collective-permute-done.6.other_ref
  35.5 0.7 %finish.1 = (f32[16,128]{1,0:T(8,128)}, f32[128,128]{1,0:T(8,128)}, f32[1,128]{1,0:T(1,128)}, f32[1,128,128]{2,1,0:T(8,128)}, f32[1,128,128]{2,1,0:T(8,128)}) custom-call(f32[80,128]{1,0:T(8,128)S(1)} %add.15.mine_ref, f32[80,128]{1,0:T(8,128)S(1)} %collective-permute-done.6.other_ref, f32[128,128]{1,0:T(8,128)S(1)} %get-tuple-element.32.source_ref, ...), custom_call_target="tpu_custom_call" | custom-call | tf_op jit(solution)/shard_map/finish/pallas_call | solution.py:395
  (4 shorter events, 0.0 us)
Async XLA Ops:
  0.6 33.1 %copy-start.2 = (bf16[2,256,256]{2,1,0:T(8,128)(2,1)S(1)}, bf16[2,256,256]{2,1,0:T(8,128)(2,1)}, u32[]{:S(2)}) copy-start(bf16[2,256,256]{2,1,0:T(8,128)(2,1)} %constant.9.clone.bcol_ref) | copy-start | bytes 786436
  14.8 5.2 %collective-permute-start.3 = (f32[128,128]{1,0:T(8,128)S(1)}, f32[128,128]{1,0:T(8,128)S(1)}, u32[]{:S(2)}, u32[]{:S(2)}) collective-permute-start(f32[128,128]{1,0:T(8,128)S(1)} %get-tuple-element.26), channel_id=1, source_target_pairs={{0,2},{2,0},{1,3},{3,1},{4,6},{6,4},{5,7},{7,5},{8,10},{10,8},{9,1... | collective-permute-start | bytes 196616 | tf_op jit(solution)/shard_map/ppermute | solution.py:410
  17.8 1.2 %collective-permute-start = (f32[80,128]{1,0:T(8,128)S(1)}, f32[80,128]{1,0:T(8,128)S(1)}, u32[]{:S(2)}, u32[]{:S(2)}) collective-permute-start(f32[80,128]{1,0:T(8,128)S(1)} %get-tuple-element.23), channel_id=1, source_target_pairs={{0,1},{1,0},{2,3},{3,2},{4,5},{5,4},{6,7},{7,6},{8,9},{9,8},{10,11... | collective-permute-start | bytes 122888 | tf_op jit(solution)/shard_map/ppermute | solution.py:410
  19.0 14.7 %copy-start = (bf16[2,224,272]{2,1,0:T(8,128)(2,1)S(1)}, bf16[2,224,272]{2,1,0:T(8,128)(2,1)}, u32[]{:S(2)}) copy-start(bf16[2,224,272]{2,1,0:T(8,128)(2,1)} %constant.8.clone.brow_ref) | copy-start | bytes 731140
  19.0 4.1 %collective-permute-start.1 = (f32[80,128]{1,0:T(8,128)S(1)}, f32[80,128]{1,0:T(8,128)S(1)}, u32[]{:S(2)}, u32[]{:S(2)}) collective-permute-start(f32[80,128]{1,0:T(8,128)S(1)} %add.12), channel_id=1, source_target_pairs={{0,2},{2,0},{1,3},{3,1},{4,6},{6,4},{5,7},{7,5},{8,10},{10,8},{9,1... | collective-permute-start | bytes 122888 | tf_op jit(solution)/shard_map/ppermute | solution.py:410
  20.0 13.7 %copy-start.1 = (f32[2,272,128]{2,1,0:T(8,128)S(1)}, f32[2,272,128]{2,1,0:T(8,128)}, u32[]{:S(2)}) copy-start(f32[2,272,128]{2,1,0:T(8,128)} %constant.10.clone.krow_ref) | copy-start | bytes 835588
  20.1 7.0 %collective-permute-start.4 = (bf16[128,256]{1,0:T(8,128)(2,1)S(1)}, bf16[128,256]{1,0:T(8,128)(2,1)S(1)}, u32[]{:S(2)}, u32[]{:S(2)}) collective-permute-start(bf16[128,256]{1,0:T(8,128)(2,1)S(1)} %get-tuple-element.27), channel_id=1, source_target_pairs={{0,4},{4,0},{8,12},{12,8},{1,5},{5,1},{9,13},{13,9},{2,6},{6,2},{1... | collective-permute-start | bytes 196616 | tf_op jit(solution)/shard_map/ppermute | solution.py:422
  23.1 4.0 %collective-permute-start.2 = (f32[80,128]{1,0:T(8,128)S(1)}, f32[80,128]{1,0:T(8,128)S(1)}, u32[]{:S(2)}, u32[]{:S(2)}) collective-permute-start(f32[80,128]{1,0:T(8,128)S(1)} %add.13), channel_id=1, source_target_pairs={{0,4},{4,0},{8,12},{12,8},{1,5},{5,1},{9,13},{13,9},{2,6},{6,2},{1... | collective-permute-start | bytes 122888 | tf_op jit(solution)/shard_map/ppermute | solution.py:410
  27.1 6.6 %copy-start.3 = (f32[8,256]{1,0:T(8,128)S(1)}, f32[8,256]{1,0:T(8,128)}, u32[]{:S(2)}) copy-start(f32[8,256]{1,0:T(8,128)} %constant.11.clone.kcol_ref) | copy-start | bytes 24580
  27.1 6.6 %collective-permute-start.7 = (bf16[128,256]{1,0:T(8,128)(2,1)S(1)}, bf16[128,256]{1,0:T(8,128)(2,1)S(1)}, u32[]{:S(2)}, u32[]{:S(2)}) collective-permute-start(bf16[128,256]{1,0:T(8,128)(2,1)S(1)} %get-tuple-element.31), channel_id=1, source_target_pairs={{4,8},{8,4},{5,9},{9,5},{6,10},{10,6},{7,11},{11,7},{20,24},{24,20... | collective-permute-start | bytes 196616 | tf_op jit(solution)/shard_map/ppermute | solution.py:422
  27.8 5.9 %collective-permute-start.5 = (f32[80,128]{1,0:T(8,128)S(1)}, f32[80,128]{1,0:T(8,128)S(1)}, u32[]{:S(2)}, u32[]{:S(2)}) collective-permute-start(f32[80,128]{1,0:T(8,128)S(1)} %add.14), channel_id=1, source_target_pairs={{0,12},{4,8},{8,4},{12,0},{1,13},{5,9},{9,5},{13,1},{2,14},{6,10},... | collective-permute-start | bytes 122888 | tf_op jit(solution)/shard_map/ppermute | solution.py:410
  33.7 1.8 %collective-permute-start.6 = (f32[80,128]{1,0:T(8,128)S(1)}, f32[80,128]{1,0:T(8,128)S(1)}, u32[]{:S(2)}, u32[]{:S(2)}) collective-permute-start(f32[80,128]{1,0:T(8,128)S(1)} %add.15.mine_ref), channel_id=1, source_target_pairs={{0,1},{1,0},{2,3},{3,2},{4,5},{5,4},{6,7},{7,6},{8,9},{9,8},{10,11... | collective-permute-start | bytes 122888 | tf_op jit(solution)/shard_map/ppermute | solution.py:410

commit v6 on v5

--- a/solution.py
+++ b/solution.py
@@ -63,6 +63,8 @@
     obf[...] = ob
     wmf[...] = wm
     mkf[...] = mk
+    tot = lambda v: jnp.sum(jnp.sum(v, axis=1, keepdims=True), axis=0, keepdims=True)
+    weight_sum, target_sum = tot(wm), tot(tg)
 
     def one(i, k, f1=True, f2=True, f3=True):
         a, b, c = k % 3, (k + 2) % 3, (k + 1) % 3
@@ -145,11 +147,10 @@
     src = src_out[...]
     og = jnp.sum(acc_outg[...].T, axis=0, keepdims=True)
     me = lax.axis_index("maps")
-    tot = lambda v: jnp.sum(jnp.sum(v, axis=1, keepdims=True), axis=0, keepdims=True)
     extra = jnp.where(sub == 0, og, 0.0)
-    extra = jnp.where(sub == 1, tot(wmf[...]), extra)
+    extra = jnp.where(sub == 1, weight_sum, extra)
     extra = jnp.where(sub == 2 + me, tot(src), extra)
-    extra = jnp.where(sub == 4 + me, tot(tgt_out[...]), extra)
+    extra = jnp.where(sub == 4 + me, target_sum, extra)
     second = acc_second[...]
     cut = hid // 2
     upper = jnp.concatenate([second[0:cut], extra, jnp.zeros((feat - 8, 128), F32)], axis=0)

time: 36.6 us -> 36.6 us (level)
  no operation moved by 1% of the time
where the time goes in v6:
time: 36.6 us; the launch traced here: 36.2 us
  Pallas kernels  16.7 us (46%)
  starting transfers between devices  11.2 us (31%)
  waiting for transfers between devices  7.52 us (21%)
  between operations  0.75 us (2%)
    pallas_call x1, Pallas kernels, net(): pl.pallas_call(functools.partial(net_kernel, sides), out_shape=[vmem(hid...  14.2 us
    ppermute x6, starting transfers between devices, swap(): lax.ppermute(value, axis, [(i, i ^ step) for i in range(lax.axis_size(axi...  8.39 us
    ppermute x6, waiting for transfers between devices, swap(): lax.ppermute(value, axis, [(i, i ^ step) for i in range(lax.axis_size(axi...  7.52 us
    ppermute x2, starting transfers between devices, exchange(): return lax.ppermute(value, axis, pairs)  2.83 us
    pallas_call x1, Pallas kernels, sinkhorn(): pl.pallas_call(sinkhorn_kernel, out_shape=[vmem(rows, cols)] * 2, compile...  1.75 us
  transfers between devices with their start and end apart: 8, of which 5 were waited for; matrix products, arithmetic and copies ran while one was open for 0% of the time, Pallas kernels for 5%

profile of v6, /device:TPU:0, one launch (start us, length us, event | category | flops | bytes accessed | tf_op | source)
XLA Modules:
  0.0 36.2 jit_solution(6326850211459553145)
XLA Ops:
  0.6 0.0 copy-start.2
  0.6 14.2 %net.1 = (f32[80,128]{1,0:T(8,128)S(1)}, f32[80,128]{1,0:T(8,128)S(1)}, f32[128,128]{1,0:T(8,128)S(1)}, f32[128,128]{1,0:T(8,128)S(1)}, f32[128,128]{1,0:T(8,128)S(1)}) custom-call(bf16[1,16,128,128]{3,2,1,0:T(8,128)(2,1)} %refs_0_.1, bf16[1,128,128]{2,1,0:T(8,128)(2,1)} %refs_1_.1, bf16[1,128,128]{2,1,0:T(8,128)(2,1)} %refs_2_.1, s32[128,128]{1,0:T(8,128)} %refs_3_.1, ...), custom_call_target="tpu_custom_call" | custom-call | tf_op jit(solution)/shard_map/net/pallas_call | solution.py:186
  14.8 3.0 %collective-permute-start.3 = (f32[128,128]{1,0:T(8,128)S(1)}, f32[128,128]{1,0:T(8,128)S(1)}, u32[]{:S(2)}, u32[]{:S(2)}) collective-permute-start(f32[128,128]{1,0:T(8,128)S(1)} %get-tuple-element.26), channel_id=1, source_target_pairs={{0,2},{2,0},{1,3},{3,1},{4,6},{6,4},{5,7},{7,5},{8,10},{10,8},{9,1... | collective-permute-start | bytes 196616 | tf_op jit(solution)/shard_map/ppermute | solution.py:411
  17.8 0.0 collective-permute-start
  17.8 1.2 %collective-permute-done = f32[80,128]{1,0:T(8,128)S(1)} collective-permute-done((f32[80,128]{1,0:T(8,128)S(1)}, f32[80,128]{1,0:T(8,128)S(1)}, u32[]{:S(2)}, u32[]{:S(2)}) %collective-permute-start) | collective-permute-done | bytes 40992 | tf_op jit(solution)/shard_map/ppermute | solution.py:411
  19.0 0.0 copy-start
  19.1 0.1 collective-permute-start.1
  19.2 0.9 %collective-permute-done.3.refs_0_ = f32[128,128]{1,0:T(8,128)S(1)} collective-permute-done((f32[128,128]{1,0:T(8,128)S(1)}, f32[128,128]{1,0:T(8,128)S(1)}, u32[]{:S(2)}, u32[]{:S(2)}) %collective-permute-start.3) | collective-permute-done | bytes 65568 | tf_op jit(solution)/shard_map/ppermute | solution.py:411
  20.1 0.0 copy-start.1
  20.1 0.1 halo.1
  20.2 2.2 %collective-permute-start.4 = (bf16[128,256]{1,0:T(8,128)(2,1)S(1)}, bf16[128,256]{1,0:T(8,128)(2,1)S(1)}, u32[]{:S(2)}, u32[]{:S(2)}) collective-permute-start(bf16[128,256]{1,0:T(8,128)(2,1)S(1)} %get-tuple-element.27), channel_id=1, source_target_pairs={{0,4},{4,0},{8,12},{12,8},{1,5},{5,1},{9,13},{13,9},{2,6},{6,2},{1... | collective-permute-start | bytes 196616 | tf_op jit(solution)/shard_map/ppermute | solution.py:423
  22.3 0.8 %collective-permute-done.1 = f32[80,128]{1,0:T(8,128)S(1)} collective-permute-done((f32[80,128]{1,0:T(8,128)S(1)}, f32[80,128]{1,0:T(8,128)S(1)}, u32[]{:S(2)}, u32[]{:S(2)}) %collective-permute-start.1) | collective-permute-done | bytes 40992 | tf_op jit(solution)/shard_map/ppermute | solution.py:411
  23.1 1.6 %collective-permute-start.2 = (f32[80,128]{1,0:T(8,128)S(1)}, f32[80,128]{1,0:T(8,128)S(1)}, u32[]{:S(2)}, u32[]{:S(2)}) collective-permute-start(f32[80,128]{1,0:T(8,128)S(1)} %add.13), channel_id=1, source_target_pairs={{0,4},{4,0},{8,12},{12,8},{1,5},{5,1},{9,13},{13,9},{2,6},{6,2},{1... | collective-permute-start | bytes 122888 | tf_op jit(solution)/shard_map/ppermute | solution.py:411
  24.7 2.4 %collective-permute-done.2 = f32[80,128]{1,0:T(8,128)S(1)} collective-permute-done((f32[80,128]{1,0:T(8,128)S(1)}, f32[80,128]{1,0:T(8,128)S(1)}, u32[]{:S(2)}, u32[]{:S(2)}) %collective-permute-start.2) | collective-permute-done | bytes 40992 | tf_op jit(solution)/shard_map/ppermute | solution.py:411
  27.1 0.0 collective-permute-done.4.pair_ref
  27.1 0.0 copy-start.3
  27.2 0.7 %collective-permute-start.7 = (bf16[128,256]{1,0:T(8,128)(2,1)S(1)}, bf16[128,256]{1,0:T(8,128)(2,1)S(1)}, u32[]{:S(2)}, u32[]{:S(2)}) collective-permute-start(bf16[128,256]{1,0:T(8,128)(2,1)S(1)} %get-tuple-element.31), channel_id=1, source_target_pairs={{4,8},{8,4},{5,9},{9,5},{6,10},{10,6},{7,11},{11,7},{20,24},{24,20... | collective-permute-start | bytes 196616 | tf_op jit(solution)/shard_map/ppermute | solution.py:423
  27.8 3.7 %collective-permute-start.5 = (f32[80,128]{1,0:T(8,128)S(1)}, f32[80,128]{1,0:T(8,128)S(1)}, u32[]{:S(2)}, u32[]{:S(2)}) collective-permute-start(f32[80,128]{1,0:T(8,128)S(1)} %add.14), channel_id=1, source_target_pairs={{0,12},{4,8},{8,4},{12,0},{1,13},{5,9},{9,5},{13,1},{2,14},{6,10},... | collective-permute-start | bytes 122888 | tf_op jit(solution)/shard_map/ppermute | solution.py:411
  31.5 2.2 %collective-permute-done.5 = f32[80,128]{1,0:T(8,128)S(1)} collective-permute-done((f32[80,128]{1,0:T(8,128)S(1)}, f32[80,128]{1,0:T(8,128)S(1)}, u32[]{:S(2)}, u32[]{:S(2)}) %collective-permute-start.5) | collective-permute-done | bytes 40992 | tf_op jit(solution)/shard_map/ppermute | solution.py:411
  33.7 0.0 collective-permute-start.6
  33.7 0.0 collective-permute-done.7.next_ref
  33.7 0.0 copy-done.2
  33.7 0.0 copy-done
  33.7 0.0 copy-done.1
  33.8 0.0 copy-done.3
  33.8 1.8 %sinkhorn.1 = (f32[128,128]{1,0:T(8,128)S(1)}, f32[128,128]{1,0:T(8,128)S(1)}) custom-call(f32[128,128]{1,0:T(8,128)S(1)} %get-tuple-element.24.src_ref, f32[128,128]{1,0:T(8,128)S(1)} %get-tuple-element.25.tgt_ref, bf16[128,256]{1,0:T(8,128)(2,1)S(1)} %collective-permute-done.4.pair_ref, bf16[128,256]{1,0:T(8,128)(2,1)S(1)} %collective-permute-done.7.next_ref, ...), custom_call_target="tpu_custom_call" | custom-call | flops 2000000000 | bytes 1000000 | tf_op jit(solution)/shard_map/sinkhorn/pallas_call | solution.py:366
  35.5 0.0 collective-permute-done.6.other_ref
  35.5 0.7 %finish.1 = (f32[16,128]{1,0:T(8,128)}, f32[128,128]{1,0:T(8,128)}, f32[1,128]{1,0:T(1,128)}, f32[1,128,128]{2,1,0:T(8,128)}, f32[1,128,128]{2,1,0:T(8,128)}) custom-call(f32[80,128]{1,0:T(8,128)S(1)} %add.15.mine_ref, f32[80,128]{1,0:T(8,128)S(1)} %collective-permute-done.6.other_ref, f32[128,128]{1,0:T(8,128)S(1)} %get-tuple-element.32.source_ref, ...), custom_call_target="tpu_custom_call" | custom-call | tf_op jit(solution)/shard_map/finish/pallas_call | solution.py:396
  (4 shorter events, 0.0 us)
Async XLA Ops:
  0.6 33.1 %copy-start.2 = (bf16[2,256,256]{2,1,0:T(8,128)(2,1)S(1)}, bf16[2,256,256]{2,1,0:T(8,128)(2,1)}, u32[]{:S(2)}) copy-start(bf16[2,256,256]{2,1,0:T(8,128)(2,1)} %constant.9.clone.bcol_ref) | copy-start | bytes 786436
  14.8 5.3 %collective-permute-start.3 = (f32[128,128]{1,0:T(8,128)S(1)}, f32[128,128]{1,0:T(8,128)S(1)}, u32[]{:S(2)}, u32[]{:S(2)}) collective-permute-start(f32[128,128]{1,0:T(8,128)S(1)} %get-tuple-element.26), channel_id=1, source_target_pairs={{0,2},{2,0},{1,3},{3,1},{4,6},{6,4},{5,7},{7,5},{8,10},{10,8},{9,1... | collective-permute-start | bytes 196616 | tf_op jit(solution)/shard_map/ppermute | solution.py:411
  17.8 1.2 %collective-permute-start = (f32[80,128]{1,0:T(8,128)S(1)}, f32[80,128]{1,0:T(8,128)S(1)}, u32[]{:S(2)}, u32[]{:S(2)}) collective-permute-start(f32[80,128]{1,0:T(8,128)S(1)} %get-tuple-element.23), channel_id=1, source_target_pairs={{0,1},{1,0},{2,3},{3,2},{4,5},{5,4},{6,7},{7,6},{8,9},{9,8},{10,11... | collective-permute-start | bytes 122888 | tf_op jit(solution)/shard_map/ppermute | solution.py:411
  19.0 14.7 %copy-start = (bf16[2,224,272]{2,1,0:T(8,128)(2,1)S(1)}, bf16[2,224,272]{2,1,0:T(8,128)(2,1)}, u32[]{:S(2)}) copy-start(bf16[2,224,272]{2,1,0:T(8,128)(2,1)} %constant.8.clone.brow_ref) | copy-start | bytes 731140
  19.1 4.1 %collective-permute-start.1 = (f32[80,128]{1,0:T(8,128)S(1)}, f32[80,128]{1,0:T(8,128)S(1)}, u32[]{:S(2)}, u32[]{:S(2)}) collective-permute-start(f32[80,128]{1,0:T(8,128)S(1)} %add.12), channel_id=1, source_target_pairs={{0,2},{2,0},{1,3},{3,1},{4,6},{6,4},{5,7},{7,5},{8,10},{10,8},{9,1... | collective-permute-start | bytes 122888 | tf_op jit(solution)/shard_map/ppermute | solution.py:411
  20.1 13.7 %copy-start.1 = (f32[2,272,128]{2,1,0:T(8,128)S(1)}, f32[2,272,128]{2,1,0:T(8,128)}, u32[]{:S(2)}) copy-start(f32[2,272,128]{2,1,0:T(8,128)} %constant.10.clone.krow_ref) | copy-start | bytes 835588
  20.2 7.0 %collective-permute-start.4 = (bf16[128,256]{1,0:T(8,128)(2,1)S(1)}, bf16[128,256]{1,0:T(8,128)(2,1)S(1)}, u32[]{:S(2)}, u32[]{:S(2)}) collective-permute-start(bf16[128,256]{1,0:T(8,128)(2,1)S(1)} %get-tuple-element.27), channel_id=1, source_target_pairs={{0,4},{4,0},{8,12},{12,8},{1,5},{5,1},{9,13},{13,9},{2,6},{6,2},{1... | collective-permute-start | bytes 196616 | tf_op jit(solution)/shard_map/ppermute | solution.py:423
  23.1 4.0 %collective-permute-start.2 = (f32[80,128]{1,0:T(8,128)S(1)}, f32[80,128]{1,0:T(8,128)S(1)}, u32[]{:S(2)}, u32[]{:S(2)}) collective-permute-start(f32[80,128]{1,0:T(8,128)S(1)} %add.13), channel_id=1, source_target_pairs={{0,4},{4,0},{8,12},{12,8},{1,5},{5,1},{9,13},{13,9},{2,6},{6,2},{1... | collective-permute-start | bytes 122888 | tf_op jit(solution)/shard_map/ppermute | solution.py:411
  27.1 6.6 %copy-start.3 = (f32[8,256]{1,0:T(8,128)S(1)}, f32[8,256]{1,0:T(8,128)}, u32[]{:S(2)}) copy-start(f32[8,256]{1,0:T(8,128)} %constant.11.clone.kcol_ref) | copy-start | bytes 24580
  27.2 6.6 %collective-permute-start.7 = (bf16[128,256]{1,0:T(8,128)(2,1)S(1)}, bf16[128,256]{1,0:T(8,128)(2,1)S(1)}, u32[]{:S(2)}, u32[]{:S(2)}) collective-permute-start(bf16[128,256]{1,0:T(8,128)(2,1)S(1)} %get-tuple-element.31), channel_id=1, source_target_pairs={{4,8},{8,4},{5,9},{9,5},{6,10},{10,6},{7,11},{11,7},{20,24},{24,20... | collective-permute-start | bytes 196616 | tf_op jit(solution)/shard_map/ppermute | solution.py:423
  27.8 5.9 %collective-permute-start.5 = (f32[80,128]{1,0:T(8,128)S(1)}, f32[80,128]{1,0:T(8,128)S(1)}, u32[]{:S(2)}, u32[]{:S(2)}) collective-permute-start(f32[80,128]{1,0:T(8,128)S(1)} %add.14), channel_id=1, source_target_pairs={{0,12},{4,8},{8,4},{12,0},{1,13},{5,9},{9,5},{13,1},{2,14},{6,10},... | collective-permute-start | bytes 122888 | tf_op jit(solution)/shard_map/ppermute | solution.py:411
  33.7 1.8 %collective-permute-start.6 = (f32[80,128]{1,0:T(8,128)S(1)}, f32[80,128]{1,0:T(8,128)S(1)}, u32[]{:S(2)}, u32[]{:S(2)}) collective-permute-start(f32[80,128]{1,0:T(8,128)S(1)} %add.15.mine_ref), channel_id=1, source_target_pairs={{0,1},{1,0},{2,3},{3,2},{4,5},{5,4},{6,7},{7,6},{8,9},{9,8},{10,11... | collective-permute-start | bytes 122888 | tf_op jit(solution)/shard_map/ppermute | solution.py:411
